TPU v7x, 512 devices: a whole 4x4x16 slice. The times are simulated.
512 devices in a mesh: dp: 64 (over x_lo, z, core), cuts: 8 (over y, x_hi).
Axes of the slice: x: 4 (x_hi: 2, x_lo: 2; x = x_hi * 2 + x_lo), y: 4, z: 16, core: 2. Of those that a mesh axis runs over, the one named last changes fastest.
Arguments:
- prompt_features: bfloat16 [16384, 1024], P('dp'), may hold values from -64 to 64
- refusal_features: bfloat16 [16384, 1024], P('dp'), may hold values from -64 to 64
- projection: bfloat16 [1024, 1024], P(None, 'cuts'), may hold values from -0.1875 to 0.1875
- positives: int32 [16384], P('dp'), may hold values from 0 to 255, as said below
Outputs:
- projection_grad: float32 [1024, 1024], P(None, 'cuts')
Inputs may be any that keep to these rules, and one draw needn't show every extreme that they name: `positives`: within each aligned block of 256 prompts, a permutation of 0 to 255.
All inputs are finite; a program needn't handle non-finite values.
Results may differ from a plain program's by a relative error of at most 0.0021.
The roundings to bfloat16 on the way count: a program that leaves them out, or rounds other values in their place, can miss the bound.
Values may be sent and summed in bfloat16 or wider, within the bound.
No kernel may reach another device: no remote copies, remote signals or barrier semaphores. Data moves between devices by JAX's collectives and lax.ppermute only.
A program may use at most 64 MiB of HBM per device.

v0:
```python
import jax
import jax.numpy as jnp
from jax import lax
from jax.sharding import PartitionSpec as P


def combined_all(x, axis, combine):
    everything = jax.tree.map(lambda part: lax.all_gather(part, axis), x)
    first = jax.tree.map(lambda part: part[0], everything)

    def lap(k, so_far):
        return combine(so_far, jax.tree.map(lambda part: part[k], everything))

    return lax.fori_loop(1, lax.axis_size(axis), lap, first)


def from_behind(x, axis, by):
    devices = lax.axis_size(axis)
    return lax.ppermute(x, axis, [(i, (i + by) % devices) for i in range(devices)])


def join_stats(first, second):
    top = jnp.maximum(first[0], second[0])
    return (top, first[1] * jnp.exp(first[0] - top) + second[1] * jnp.exp(second[0] - top))


def shards(prompt_features, refusal_features, projection, positives):
    rows = prompt_features.shape[0]
    width = projection.shape[1] * lax.axis_size("cuts")
    inv_scale = width ** (-0.5)
    groups = lax.axis_size("dp")
    dp_index = lax.axis_index("dp")
    cut_index = lax.axis_index("cuts")
    prompt_cols = jnp.dot(prompt_features, projection, preferred_element_type=jnp.float32).astype(
        jnp.bfloat16
    )
    refusal_cols = jnp.dot(refusal_features, projection, preferred_element_type=jnp.float32).astype(
        jnp.bfloat16
    )
    queries = lax.all_gather(prompt_cols, "cuts", axis=1, tiled=True)
    key_rows = lax.all_to_all(refusal_cols, "cuts", split_axis=0, concat_axis=1, tiled=True)
    block = key_rows.shape[0]
    all_keys = lax.all_gather(key_rows, "dp", axis=0, tiled=True)
    scores = (
        lax.dot_general(
            all_keys, queries, (((1,), (1,)), ((), ())), preferred_element_type=jnp.float32
        )
        * inv_scale
    )
    row_top = jnp.max(scores, axis=0)
    row_total = jnp.sum(jnp.exp(scores - row_top[None, :]), axis=0)
    row_top, row_total = combined_all((row_top, row_total), "cuts", join_stats)
    row_lse = row_top + jnp.log(row_total)
    col_top = jnp.max(scores, axis=1)
    col_total = jnp.sum(jnp.exp(scores - col_top[:, None]), axis=1)
    col_top, col_total = combined_all((col_top, col_total), "dp", join_stats)
    col_lse = col_top + jnp.log(col_total)
    probs = jnp.exp(scores - row_lse[None, :]) + jnp.exp(scores - col_lse[:, None])
    own_rows = lax.dynamic_slice_in_dim(probs, dp_index * block, block, 0)
    marks = (
        positives[None, :] == cut_index * block + jnp.arange(block, dtype=jnp.int32)[:, None]
    ).astype(jnp.float32)
    probs = lax.dynamic_update_slice_in_dim(probs, own_rows - 2.0 * marks, dp_index * block, 0)
    grads = (probs / (2.0 * (rows * groups))).astype(jnp.bfloat16)
    prompt_full = (
        lax.dot_general(
            grads, all_keys, (((0,), (0,)), ((), ())), preferred_element_type=jnp.float32
        )
        * inv_scale
    )
    prompt_grad = lax.psum_scatter(prompt_full, "cuts", scatter_dimension=1, tiled=True).astype(
        jnp.bfloat16
    )

    def partial_rows(start, count):
        piece = lax.dynamic_slice_in_dim(grads, start, count, 0)
        return jnp.dot(piece, queries, preferred_element_type=jnp.float32) * inv_scale

    def advance(turn, running):
        running = from_behind(running, "dp", 1)
        target = (dp_index - turn - 1 + 2 * groups) % groups
        return running + partial_rows(target * block, block)

    start_block = (dp_index - 1 + groups) % groups
    key_grad = lax.fori_loop(1, groups, advance, partial_rows(start_block * block, block))
    refusal_grad = lax.all_to_all(
        key_grad.astype(jnp.bfloat16), "cuts", split_axis=1, concat_axis=0, tiled=True
    )
    local_grad = lax.dot_general(
        prompt_features, prompt_grad, (((0,), (0,)), ((), ())), preferred_element_type=jnp.float32
    )
    local_grad = local_grad + lax.dot_general(
        refusal_features, refusal_grad, (((0,), (0,)), ((), ())), preferred_element_type=jnp.float32
    )
    return lax.psum(local_grad, "dp")


def solution(mesh):
    placed = (P("dp", None), P("dp", None), P(None, "cuts"), P("dp"))
    return jax.shard_map(
        shards, mesh=mesh, in_specs=placed, out_specs=P(None, "cuts"), check_vma=False
    )
```

profile of v0, /device:TPU:1, one launch (start us, length us, event | category | flops | bytes accessed | tf_op | source)
XLA Modules:
  0.0 1377.7 jit_solution(5634983064585577713)
XLA Ops:
  8.0 14.1 %all_to_all.38 = bf16[8,32,128]{2,1,0:T(8,128)(2,1)S(1)} all-to-all(bf16[8,32,128]{2,1,0:T(8,128)(2,1)S(1)} %bitcast.57), channel_id=1, replica_groups=mesh['dp'=64,'cuts'=8] {'cuts'}, dimensions={0} | all-to-all | bytes 131072 | tf_op jit(solution)/shard_map/all_to_all | solution.py:41
  24.1 28.4 %all_gather.31 = bf16[256,1024]{1,0:T(8,128)(2,1)S(1)} all-gather(bf16[256,128]{1,0:T(8,128)(2,1)S(1)} %convolution_convert_fusion), channel_id=1, replica_groups=mesh['dp'=64,'cuts'=8] {'cuts'}, dimensions={1}, use_global_device_ids=true | all-gather | bytes 589824 | tf_op jit(solution)/shard_map/all_gather | solution.py:40
  52.5 96.6 %all-gather.8.cloned.1.call-done = bf16[2048,1024]{1,0:T(8,128)(2,1)} async-done(((bf16[32,1024]{1,0:T(8,128)(2,1)}), bf16[2048,1024]{1,0:T(8,128)(2,1)}) %all-gather.8.cloned.1.call-update) | async-done | bytes 4194320 | tf_op jit(solution)/shard_map/all_gather | solution.py:43
  153.5 19.6 %all-gather.5 = f32[8,1,256]{2,1,0:T(1,128)S(1)} all-gather(f32[1,1,256]{2,1,0:T(1,128)S(1)} %bitcast.65), channel_id=3, replica_groups=mesh['dp'=64,'cuts'=8] {'cuts'}, dimensions={0}, use_global_device_ids=true | all-gather | bytes 9216 | tf_op jit(solution)/shard_map/all_gather | solution.py:8
  173.1 14.6 %all-gather.4 = f32[8,1,256]{2,1,0:T(1,128)S(1)} all-gather(f32[1,1,256]{2,1,0:T(1,128)S(1)} %bitcast.64), channel_id=2, replica_groups=mesh['dp'=64,'cuts'=8] {'cuts'}, dimensions={0}, use_global_device_ids=true | all-gather | bytes 9216 | tf_op jit(solution)/shard_map/all_gather | solution.py:8
  187.7 75.1 %all-gather.3 = f32[131072]{0:T(1024)} all-gather(f32[2048]{0:T(1024)S(1)} %get-tuple-element.449), channel_id=5, replica_groups=mesh['dp'=64,'cuts'=8] {'dp'}, dimensions={0}, use_global_device_ids=true | all-gather | bytes 532480 | tf_op jit(solution)/shard_map/all_gather | solution.py:8
  264.9 66.1 %all-gather.2 = f32[131072]{0:T(1024)} all-gather(f32[2048]{0:T(1024)S(1)} %get-tuple-element.451), channel_id=4, replica_groups=mesh['dp'=64,'cuts'=8] {'dp'}, dimensions={0}, use_global_device_ids=true | all-gather | bytes 532480 | tf_op jit(solution)/shard_map/all_gather | solution.py:8
  334.0 58.8 %while.52 = (s32[]{:T(128)}, f32[2048]{0:T(1024)S(1)}, f32[2048]{0:T(1024)S(1)}, f32[64,2048]{1,0:T(8,128)}, f32[64,2048]{1,0:T(8,128)}, /*index=5*/s32[]{:T(128)}, s32[]{:T(128)}, s32[]{:T(128)}) while((s32[]{:T(128)}, f32[2048]{0:T(1024)S(1)}, f32[2048]{0:T(1024)S(1)}, f32[64,2048]{1,0:T(8,128)}, f32[64,2048]{1,0:T(8,128)}, ...), condition=%wide.region_7.0_spmd, body=%wide.region_6.0_spmd.sunk | while | flops 12293 | bytes 82051 | solution.py:14
  397.3 536.5 %while.53 = (s32[]{:T(128)}, f32[32,1024]{1,0:T(8,128)S(1)}, s32[]{:T(128)}, bf16[2048,256]{1,0:T(8,128)(2,1)S(1)}, bf16[256,1024]{1,0:T(8,128)(2,1)S(1)}, /*ind...) while((s32[]{:T(128)}, f32[32,1024]{1,0:T(8,128)S(1)}, ...), condition=%wide.region_10.11_spmd, body=%wide.region_9.10_spmd.sunk | while | flops 16842772 | bytes 1327444 | solution.py:85
  428.4 6.5 collective-permute-done
  437.0 6.4 collective-permute-done
  445.7 6.4 collective-permute-done
  454.3 6.4 collective-permute-done
  462.9 6.4 collective-permute-done
  471.4 6.4 collective-permute-done
  480.0 6.4 collective-permute-done
  488.6 6.4 collective-permute-done
  497.2 6.4 collective-permute-done
  514.4 6.4 collective-permute-done
  523.0 6.4 collective-permute-done
  531.6 6.4 collective-permute-done
  540.2 6.4 collective-permute-done
  548.8 6.4 collective-permute-done
  557.4 6.4 collective-permute-done
  566.0 6.4 collective-permute-done
  574.6 6.4 collective-permute-done
  583.2 6.4 collective-permute-done
  591.8 6.4 collective-permute-done
  609.0 6.4 collective-permute-done
  617.6 6.4 collective-permute-done
  626.2 6.4 collective-permute-done
  947.2 421.9 %all-reduce.2.cloned.1.call-done = f32[1024,128]{0,1:T(8,128)} async-done(((f32[1024,128]{0,1:T(8,128)}), f32[1024,128]{0,1:T(8,128)}) %all-reduce.2.cloned.1.call-update) | async-done | bytes 524304 | tf_op jit(solution)/shard_map/psum | solution.py:95
  (351 shorter events, 481.8 us)
Async XLA Ops:
  6.5 142.5 %all-gather.8.cloned.1.call-start = ((), (), s32[]{:S(2)}) async-start(), calls=%async_computation.3 | async-start | bytes 4259840 | tf_op jit(solution)/shard_map/all_gather | solution.py:43
  22.7 916.8 %reduce-scatter.2.cloned.1.call-start = ((), (), s32[]{:S(2)}) async-start(), calls=%async_computation.4 | async-start | bytes 1179648 | tf_op jit(solution)/shard_map/reduce_scatter | solution.py:71
  417.8 8.4 collective-permute-start
  426.4 8.5 collective-permute-start
  435.1 8.4 collective-permute-start
  443.7 8.4 collective-permute-start
  452.3 8.4 collective-permute-start
  460.9 8.4 collective-permute-start
  469.5 8.4 collective-permute-start
  486.7 8.4 collective-permute-start
  495.3 8.4 collective-permute-start
  512.5 8.4 collective-permute-start
  521.1 8.4 collective-permute-start
  529.7 8.4 collective-permute-start
  538.3 8.4 collective-permute-start
  546.9 8.4 collective-permute-start
  555.5 8.4 collective-permute-start
  564.1 8.4 collective-permute-start
  581.3 8.4 collective-permute-start
  589.9 8.4 collective-permute-start
  607.1 8.4 collective-permute-start
  615.7 8.4 collective-permute-start
  624.3 8.4 collective-permute-start
  632.9 8.4 collective-permute-start
  650.1 8.4 collective-permute-start
  658.7 8.4 collective-permute-start
  675.9 8.4 collective-permute-start
  684.5 8.4 collective-permute-start
  693.1 8.4 collective-permute-start
  701.7 8.4 collective-permute-start
  934.5 11.6 all-to-all-start.1
  939.4 429.7 %all-reduce.2.cloned.1.call-start = ((), (), s32[]{:S(2)}) async-start(), calls=%async_computation.5 | async-start | bytes 1048576 | tf_op jit(solution)/shard_map/psum | solution.py:95
  (40 other events, 927.6 us)
Sparse Core Ops, SparseCore 0:
  22.9 126.1 all-gather.7
  397.4 76.6 reduce-scatter.1
  947.3 421.7 all-reduce.1
where the time goes:
time: 1380 us
  waiting for transfers between devices  918 us (67%)
  blocking collectives  218 us (16%)
  starting transfers between devices  133 us (10%)
  local copies, waits for them, and re-layouts  64.6 us (5%)
  matrix products  23.1 us (2%)
    psum x1, waiting for transfers between devices, shards(): return lax.psum(local_grad, 'dp')  422 us
    ppermute x63, waiting for transfers between devices, from_behind(): lax.ppermute(x, axis, [(i, (i + by) % devices) for i in range(devices)])  394 us
    all_gather x4, blocking collectives, combined_all(): everything = jax.tree.map(lambda part: lax.all_gather(part, axis), x)  175 us
    ppermute x63, starting transfers between devices, from_behind(): lax.ppermute(x, axis, [(i, (i + by) % devices) for i in range(devices)])  128 us
    all_gather x1, waiting for transfers between devices, shards(): all_keys = lax.all_gather(key_rows, 'dp', axis=0, tiled=True)  96.6 us
    dynamic_slice x70, local copies, waits for them, and re-layouts, lap(): return combine(so_far, jax.tree.map(lambda part: part[k], everything))  56.2 us
    all_gather x1, blocking collectives, shards(): queries = lax.all_gather(prompt_cols, 'cuts', axis=1, tiled=True)  28.4 us
  transfers between devices with their start and end apart: 67, of which 66 were waited for; matrix products, arithmetic and copies ran while one was open for 1% of the time, Pallas kernels for 0%

commit v1 on v0

v1 whole, which is shorter than its diff:
```python
import jax
import jax.numpy as jnp
from jax import lax
from jax.sharding import Mesh, PartitionSpec as P

DP = ("x_lo", "z", "core")
CUTS = ("y", "x_hi")
PLANE = ("core", "x_lo", "y", "x_hi")
SPREAD = ("x_lo", "y", "x_hi")


def exchange(x, axes):
    return lax.all_to_all(x, axes, split_axis=0, concat_axis=0, tiled=True)


def from_all(x, axes):
    return exchange(jnp.broadcast_to(x[None], (lax.axis_size(axes), *x.shape)), axes)


def from_twin(x, axis):
    return lax.ppermute(x, axis, [(0, 1), (1, 0)])


def from_ahead(x, axis, by):
    devices = lax.axis_size(axis)
    return lax.ppermute(x, axis, [((i + by) % devices, i) for i in range(devices)])


def in_order(mine, other, axis, dimension):
    first = lax.axis_index(axis) == 0
    return jnp.concatenate(
        [jnp.where(first, mine, other), jnp.where(first, other, mine)], dimension
    )


def whole_projection(projection):
    half = projection.shape[0] // 2
    own = lax.dynamic_slice_in_dim(projection, lax.axis_index("core") * half, half, 0)
    strip = in_order(own, from_twin(own, "x_hi"), "x_hi", 1)
    turns, at = lax.axis_size("y"), lax.axis_index("y")
    strips = [strip] + [from_ahead(strip, "y", by) for by in range(1, turns)]
    lap = jnp.concatenate(strips + strips, 1)
    start = (turns - at) % turns * strip.shape[1]
    mine = lax.dynamic_slice_in_dim(lap, start, turns * strip.shape[1], 1)
    return in_order(mine, from_twin(mine, "core"), "core", 0)


def log_sum_exp(x, axis):
    top = jnp.max(x, axis=axis, keepdims=True)
    total = jnp.sum(jnp.exp(x - top), axis=axis)
    return jnp.squeeze(top, axis) + jnp.log(total)


def own_first(x):
    x = jnp.where(lax.axis_index("core") == 1, x[::-1], x)
    return jnp.where(lax.axis_index("x_lo") == 1, x[:, ::-1], x)


def in_two(x):
    high = lax.reduce_precision(x, 8, 7)
    return high.astype(jnp.bfloat16), (x - high).astype(jnp.bfloat16)


def dot_first(a, b):
    return lax.dot_general(a, b, (((0,), (0,)), ((), ())), preferred_element_type=jnp.float32)


def shards(prompt_features, refusal_features, projection, positives):
    rows, depth = prompt_features.shape
    cuts = lax.axis_size(CUTS)
    width = projection.shape[1] * cuts
    pairs = rows * lax.axis_size(DP)
    inv_scale = width ** (-0.5)
    cut = lax.axis_index(CUTS)
    layer = lax.axis_index("z")
    chunk = rows // cuts

    own = lax.dynamic_slice_in_dim(refusal_features, cut * chunk, chunk, 0)
    refusals = from_all(own, "z").reshape(-1, depth)
    whole = whole_projection(projection)
    beside = from_twin(prompt_features, "x_lo")
    pair_of_shards = jnp.concatenate([prompt_features, beside], 0)
    prompts = jnp.concatenate([pair_of_shards, from_twin(pair_of_shards, "core")], 0)

    prompt_emb = jnp.dot(prompts, whole, preferred_element_type=jnp.float32).astype(jnp.bfloat16)
    refusal_emb = jnp.dot(refusals, whole, preferred_element_type=jnp.float32).astype(jnp.bfloat16)
    scores = (
        lax.dot_general(
            refusal_emb, prompt_emb, (((1,), (1,)), ((), ())), preferred_element_type=jnp.float32
        )
        * inv_scale
    )
    n_keys, n_queries = scores.shape

    col_part = log_sum_exp(scores, 1).reshape(-1, 128)
    col_lse = log_sum_exp(from_all(col_part, "z"), 0).reshape(n_keys)
    row_part = own_first(log_sum_exp(scores, 0).reshape(2, 2, rows)).reshape(-1, 128)
    row_part = log_sum_exp(from_all(row_part, PLANE), 0)
    row_lse = own_first(row_part.reshape(2, 2, rows)).reshape(n_queries)

    pair = jnp.concatenate([positives, jnp.full((n_queries - rows,), -1, jnp.int32)])
    key = jnp.arange(n_keys, dtype=jnp.int32)
    place = jnp.where(key // chunk == layer, cut * chunk + key % chunk, -2)
    marks = (pair[None, :] == place[:, None]).astype(jnp.float32)
    probs = jnp.exp(scores - row_lse[None, :]) + jnp.exp(scores - col_lse[:, None])
    grads = ((probs - 2.0 * marks) / (2.0 * pairs)).astype(jnp.bfloat16)

    prompt_grad = in_two(dot_first(grads, refusal_emb) * inv_scale)
    refusal_grad = in_two(
        jnp.dot(grads, prompt_emb, preferred_element_type=jnp.float32) * inv_scale
    )

    def product(start, count):
        left = lax.dynamic_slice_in_dim(prompts, start, count, 1)
        right = lax.dynamic_slice_in_dim(refusals, start, count, 1)
        return (
            dot_first(left, prompt_grad[0])
            + dot_first(right, refusal_grad[0])
            + (dot_first(left, prompt_grad[1]) + dot_first(right, refusal_grad[1]))
        )

    core = lax.axis_index("core")
    half = depth // 2
    came = from_twin(product((1 - core) * half, half), "core")
    kept = (product(core * half, half) + came).astype(jnp.bfloat16)
    parts = lax.axis_size("x_lo")
    pieces = kept.reshape(parts, half // parts, cuts, width // cuts).transpose(0, 2, 1, 3)
    pieces = pieces.reshape(parts * cuts, half // parts, width // cuts)
    in_layer = jnp.sum(exchange(pieces, SPREAD).astype(jnp.float32), axis=0)
    slices = in_layer.reshape(lax.axis_size("z"), -1, width // cuts)
    done = jnp.sum(exchange(slices, "z"), axis=0)
    block = from_all(done, "z").reshape(in_layer.shape)
    return lax.all_gather(block, ("core", "x_lo"), axis=0, tiled=True)


def solution(mesh):
    split = Mesh(mesh.devices.reshape(2, 16, 2, 4, 2), ("x_lo", "z", "core", "y", "x_hi"))
    placed = (P(DP, None), P(DP, None), P(None, CUTS), P(DP))
    return jax.shard_map(
        shards, mesh=split, in_specs=placed, out_specs=P(None, CUTS), check_vma=False
    )
```

time: 1380 us -> 203 us (0.15)
  waiting for transfers between devices: 918 us -> 28.4 us
  blocking collectives: 218 us -> 66.7 us
  starting transfers between devices: 133 us -> 56.8 us
  local copies, waits for them, and re-layouts: 64.6 us -> 19.8 us
    psum x1 -> x0, waiting for transfers between devices: 422 us -> none  [shards(): return lax.psum(local_grad, 'dp')]
    ppermute x63 -> x8, waiting for transfers between devices: 394 us -> 9.46 us  [the longest x3 8.67 us: from_ahead(): lax.ppermute(x, axis, [((i + by) % devices, i) for i in range(devices)])]
    all_gather x5 -> x1, blocking collectives: 204 us -> 16.1 us  [shards(): return lax.all_gather(block, ('core', 'x_lo'), axis=0, tiled=True)]
    ppermute x63 -> x8, starting transfers between devices: 128 us -> 24.4 us  [the longest x5 14.9 us: from_twin(): return lax.ppermute(x, axis, [(0, 1), (1, 0)])]
    all_gather x1 -> x0, waiting for transfers between devices: 96.6 us -> none  [shards(): all_keys = lax.all_gather(key_rows, 'dp', axis=0, tiled=True)]
    dynamic_slice x70 -> x3, local copies, waits for them, and re-layouts: 56.2 us -> 3.3 us  [the longest x1 2.3 us: whole_projection(): mine = lax.dynamic_slice_in_dim(lap, start, turns * strip.shape[1], 1)]
    all_to_all x1 -> x3, blocking collectives: 14.1 us -> 50.6 us  [exchange(): return lax.all_to_all(x, axes, split_axis=0, concat_axis=0, tiled=True)]
    all_to_all x1 -> x3, starting transfers between devices: 4.95 us -> 32.5 us  [exchange(): return lax.all_to_all(x, axes, split_axis=0, concat_axis=0, tiled=True)]
  transfers between devices with their start and end apart: 67 -> 11, of which waited for: 66 -> 5; matrix products, arithmetic and copies ran while one was open for 1% -> 13% of each run, Pallas kernels for 0% -> 0%
where the time goes in v1:
time: 203 us; the launch traced here: 202 us
  blocking collectives  66.7 us (33%)
  starting transfers between devices  56.8 us (28%)
  waiting for transfers between devices  28.4 us (14%)
  matrix products  21.8 us (11%)
  local copies, waits for them, and re-layouts  19.8 us (10%)
  other arithmetic  7.65 us (4%)
    all_to_all x3, blocking collectives, exchange(): return lax.all_to_all(x, axes, split_axis=0, concat_axis=0, tiled=True)  50.6 us
    all_to_all x3, starting transfers between devices, exchange(): return lax.all_to_all(x, axes, split_axis=0, concat_axis=0, tiled=True)  32.5 us
    all_to_all x3, waiting for transfers between devices, exchange(): return lax.all_to_all(x, axes, split_axis=0, concat_axis=0, tiled=True)  18.9 us
    all_gather x1, blocking collectives, shards(): return lax.all_gather(block, ('core', 'x_lo'), axis=0, tiled=True)  16.1 us
    ppermute x5, starting transfers between devices, from_twin(): return lax.ppermute(x, axis, [(0, 1), (1, 0)])  14.9 us
    unnamed x36, local copies, waits for them, and re-layouts  10.7 us
    dot_general x9, matrix products, dot_first(): lax.dot_general(a, b, (((0,), (0,)), ((), ())), preferred_element_type=jn...  10.1 us
    ppermute x3, starting transfers between devices, from_ahead(): lax.ppermute(x, axis, [((i + by) % devices, i) for i in range(devices)])  9.49 us
  transfers between devices with their start and end apart: 11, of which 5 were waited for; matrix products, arithmetic and copies ran while one was open for 13% of the time, Pallas kernels for 0%

profile of v1, /device:TPU:1, one launch (start us, length us, event | category | flops | bytes accessed | tf_op | source)
XLA Modules:
  0.0 201.7 jit_solution(14165893973164383886)
XLA Ops:
  1.0 5.5 %collective-permute-start.2 = (bf16[512,128]{1,0:T(8,128)(2,1)S(1)}, bf16[512,128]{1,0:T(8,128)(2,1)S(1)}, u32[]{:S(2)}, u32[]{:S(2)}) collective-permute-start(bf16[512,128]{1,0:T(8,128)(2,1)S(1)} %constant_dynamic-slice_fusion.1), channel_id=1, source_target_pairs={{0,1},{1,0},{2,3},{3,2},{4,5},{5,4},{6,7},{7,6},{8,9},{9,8},{10,11... | collective-permute-start | bytes 393224 | tf_op jit(solution)/shard_map/ppermute | solution.py:21
  7.6 15.0 %all-to-all-start = ((bf16[16,32,1024]{2,1,0:T(8,128)(2,1)}), bf16[16,32,1024]{2,1,0:T(8,128)(2,1)S(1)}, u32[]{:S(2)}, u32[]{:S(2)}) async-start(bf16[16,32,1024]{2,1,0:T(8,128)(2,1)} %broadcast_in_dim.13), calls=%async_computation | async-start | bytes 2097152 | tf_op jit(solution)/shard_map/all_to_all | solution.py:13
  24.9 4.6 %collective-permute-start.3 = (bf16[512,256]{1,0:T(8,128)(2,1)}, bf16[512,256]{1,0:T(8,128)(2,1)S(1)}, u32[]{:S(2)}, u32[]{:S(2)}) collective-permute-start(bf16[512,256]{1,0:T(8,128)(2,1)} %pad_maximum_fusion.4), channel_id=1, source_target_pairs={{2,0},{4,2},{6,4},{0,6},{3,1},{5,3},{7,5},{1,7},{10,8},{12,10},{14... | collective-permute-start | bytes 786440 | tf_op jit(solution)/shard_map/ppermute | solution.py:26
  29.5 2.3 %collective-permute-start.4 = (bf16[512,256]{1,0:T(8,128)(2,1)}, bf16[512,256]{1,0:T(8,128)(2,1)S(1)}, u32[]{:S(2)}, u32[]{:S(2)}) collective-permute-start(bf16[512,256]{1,0:T(8,128)(2,1)} %pad_maximum_fusion.4), channel_id=1, source_target_pairs={{4,0},{6,2},{0,4},{2,6},{5,1},{7,3},{1,5},{3,7},{12,8},{14,10},{8,... | collective-permute-start | bytes 786440 | tf_op jit(solution)/shard_map/ppermute | solution.py:26
  31.8 2.6 %collective-permute-start.5 = (bf16[512,256]{1,0:T(8,128)(2,1)}, bf16[512,256]{1,0:T(8,128)(2,1)}, u32[]{:S(2)}, u32[]{:S(2)}) collective-permute-start(bf16[512,256]{1,0:T(8,128)(2,1)} %pad_maximum_fusion.4), channel_id=1, source_target_pairs={{6,0},{0,2},{2,4},{4,6},{7,1},{1,3},{3,5},{5,7},{14,8},{8,10},{10,... | collective-permute-start | bytes 786440 | tf_op jit(solution)/shard_map/ppermute | solution.py:26
  34.4 2.2 %collective-permute-start = (bf16[256,1024]{1,0:T(8,128)(2,1)S(1)}, bf16[256,1024]{1,0:T(8,128)(2,1)S(1)}, u32[]{:S(2)}, u32[]{:S(2)}) collective-permute-start(bf16[256,1024]{1,0:T(8,128)(2,1)S(1)} %copy-done.5), channel_id=1, source_target_pairs={{0,256},{256,0},{1,257},{257,1},{2,258},{258,2},{3,259},{259,3},{4... | collective-permute-start | bytes 1572872 | tf_op jit(solution)/shard_map/ppermute | solution.py:21
  37.4 2.0 collective-permute-done.4
  40.2 6.7 %collective-permute-done.5 = bf16[512,256]{1,0:T(8,128)(2,1)} collective-permute-done((bf16[512,256]{1,0:T(8,128)(2,1)}, bf16[512,256]{1,0:T(8,128)(2,1)}, u32[]{:S(2)}, u32[]{:S(2)}) %collective-permute-start.5) | collective-permute-done | bytes 262176 | tf_op jit(solution)/shard_map/ppermute | solution.py:26
  46.8 1.7 constant_dynamic-update-slice_fusion.8
  51.3 1.7 constant_dynamic-update-slice_fusion.3
  53.1 2.3 %constant_dynamic-slice_fusion = bf16[512,1024]{1,0:T(8,128)(2,1)} fusion(bf16[512,2048]{1,0:T(8,128)(2,1)} %constant_dynamic-update-slice_fusion.3, s32[]{:T(128)S(6)} %select_n.102), kind=kLoop, calls=%fused_computation.82 | loop fusion | bytes 2097156 | tf_op jit(solution)/shard_map/dynamic_slice | solution.py:44
  55.4 2.6 %collective-permute-start.6 = (bf16[512,1024]{1,0:T(8,128)(2,1)}, bf16[512,1024]{1,0:T(8,128)(2,1)}, u32[]{:S(2)}, u32[]{:S(2)}) collective-permute-start(bf16[512,1024]{1,0:T(8,128)(2,1)} %constant_dynamic-slice_fusion), channel_id=1, source_target_pairs={{0,8},{8,0},{1,9},{9,1},{2,10},{10,2},{3,11},{11,3},{4,12},{12,4},... | collective-permute-start | bytes 3145736 | tf_op jit(solution)/shard_map/ppermute | solution.py:21
  59.1 1.9 collective-permute-start.1
  61.1 2.0 %broadcast_select_fusion.1 = (bf16[512,1024]{1,0:T(8,128)(2,1)S(1)}, bf16[512,1024]{1,0:T(8,128)(2,1)S(1)}) fusion(bf16[512,1024]{1,0:T(8,128)(2,1)} %collective-permute-done.6, pred[]{:T(512)S(6)} %eq.41, bf16[512,2048]{1,0:T(8,128)(2,1)} %constant_dynamic-update-slice_fusion.3, s32[]{:T(128)S(6)} %select_n.102), kind=kLoop, calls=%fused_computation.19 | loop fusion | flops 1048576 | bytes 4194309 | tf_op jit(solution)/shard_map/jit(_where)/select_n | solution.py:32
  65.3 1.3 copy-done.1
  66.6 3.7 %convolution_convert_fusion = bf16[1024,1024]{1,0:T(8,128)(2,1)} fusion(bf16[1024,1024]{1,0:T(8,128)(2,1)S(1)} %constant_dynamic-update-slice_fusion, bf16[512,1024]{1,0:T(8,128)(2,1)S(1)} %get-tuple-element.14, bf16[512,1024]{1,0:T(8,128)(2,1)S(1)} %get-tuple-element.13), kind=kOutput, calls=%fused_computation.13 | convolution fusion | flops 2152726528 | bytes 6291456 | tf_op jit(solution)/shard_map/dot_general | solution.py:85
  70.3 2.6 %convolution_convert_fusion.1 = bf16[512,1024]{1,0:T(8,128)(2,1)S(1)} fusion(bf16[512,1024]{1,0:T(8,128)(2,1)S(1)} %bitcast.23, bf16[512,1024]{1,0:T(8,128)(2,1)} %copy-done.6, bf16[512,1024]{1,0:T(8,128)(2,1)S(1)} %get-tuple-element.13), kind=kOutput, calls=%fused_computation.15 | convolution fusion | flops 1078460416 | bytes 4194304 | tf_op jit(solution)/shard_map/dot_general | solution.py:86
  72.9 1.4 fusion.52
  74.3 1.3 copy-done.3
  77.0 11.5 %all-to-all-start.2 = ((f32[16,4,128]{2,1,0:T(4,128)}), f32[16,4,128]{2,1,0:T(4,128)S(1)}, u32[]{:S(2)}, u32[]{:S(2)}) async-start(f32[16,4,128]{2,1,0:T(4,128)} %broadcast_in_dim.17), calls=%async_computation.2 | async-start | bytes 65536 | tf_op jit(solution)/shard_map/all_to_all | solution.py:13
  88.6 11.4 %all-to-all-done.2 = f32[16,4,128]{2,1,0:T(4,128)S(1)} async-done(((f32[16,4,128]{2,1,0:T(4,128)}), f32[16,4,128]{2,1,0:T(4,128)S(1)}, u32[]{:S(2)}, u32[]{:S(2)}) %all-to-all-start.2) | async-done | bytes 32800 | tf_op jit(solution)/shard_map/all_to_all | solution.py:13
  100.7 6.0 %all-to-all-start.1 = ((f32[32,8,128]{2,1,0:T(8,128)}), f32[32,8,128]{2,1,0:T(8,128)S(1)}, u32[]{:S(2)}, u32[]{:S(2)}) async-start(f32[32,8,128]{2,1,0:T(8,128)} %broadcast_in_dim.15), calls=%async_computation.1 | async-start | bytes 262144 | tf_op jit(solution)/shard_map/all_to_all | solution.py:13
  106.8 7.5 %all-to-all-done.1 = f32[32,8,128]{2,1,0:T(8,128)S(1)} async-done(((f32[32,8,128]{2,1,0:T(8,128)}), f32[32,8,128]{2,1,0:T(8,128)S(1)}, u32[]{:S(2)}, u32[]{:S(2)}) %all-to-all-start.1) | async-done | bytes 131104 | tf_op jit(solution)/shard_map/all_to_all | solution.py:13
  114.5 4.0 %fusion.50 = f32[512,1024]{1,0:T(8,128)S(1)} fusion(bf16[1024,1024]{1,0:T(8,128)(2,1)} %convolution_convert_fusion, f32[512,1024]{1,0:T(8,128)} %copy-done.3, s32[1024]{0:T(1024)S(1)} %concatenate.25, f32[512]{0:T(512)S(1)} %add_bitcast_fusion, f32[1024]{0:T(1024)S(1)} %bitcast.32, s32[512]{0:T(512)S(1)} %fusion.28), kind=kOutput, calls=%fused_computation.96 | convolution fusion | flops 1077936128 | bytes 6303744 | tf_op jit(solution)/shard_map/dot_general | solution.py:110
  118.6 1.8 fusion.51
  125.3 2.6 %collective-permute-start.7 = (f32[512,1024]{1,0:T(8,128)S(1)}, f32[512,1024]{1,0:T(8,128)S(1)}, u32[]{:S(2)}, u32[]{:S(2)}) collective-permute-start(f32[512,1024]{1,0:T(8,128)S(1)} %add_add_fusion), channel_id=1, source_target_pairs={{0,8},{8,0},{1,9},{9,1},{2,10},{10,2},{3,11},{11,3},{4,12},{12,4},... | collective-permute-start | bytes 6291464 | tf_op jit(solution)/shard_map/ppermute | solution.py:21
  129.6 1.3 fusion.8
  130.9 1.3 fusion.6
  134.0 18.9 %all_to_all.30 = bf16[16,256,128]{2,1,0:T(8,128)(2,1)S(1)} all-to-all(bf16[16,256,128]{2,1,0:T(8,128)(2,1)S(1)} %bitcast.29), channel_id=1, replica_groups=mesh['x_lo'=2,'z'=16,'core'=2,'y'=4,'x_hi'=2] {'x_lo','y','x_hi'}, dimensions={0} | all-to-all | bytes 2097152 | tf_op jit(solution)/shard_map/all_to_all | solution.py:13
  153.0 14.5 %all_to_all.31 = f32[16,16,128]{2,1,0:T(8,128)S(1)} all-to-all(f32[16,16,128]{2,1,0:T(8,128)S(1)} %bitcast.30), channel_id=1, replica_groups=mesh['x_lo'=2,'z'=16,'core'=2,'y'=4,'x_hi'=2] {'z'}, dimensions={0} | all-to-all | bytes 262144 | tf_op jit(solution)/shard_map/all_to_all | solution.py:13
  167.6 17.1 %all_to_all.32 = f32[16,16,128]{2,1,0:T(8,128)S(1)} all-to-all(f32[16,16,128]{2,1,0:T(8,128)S(1)} %broadcast_in_dim.19), channel_id=1, replica_groups=mesh['x_lo'=2,'z'=16,'core'=2,'y'=4,'x_hi'=2] {'z'}, dimensions={0} | all-to-all | bytes 262144 | tf_op jit(solution)/shard_map/all_to_all | solution.py:13
  184.7 16.1 %all_gather.3 = f32[1024,128]{1,0:T(8,128)S(1)} all-gather(f32[256,128]{1,0:T(8,128)S(1)} %bitcast.31), channel_id=1, replica_groups=mesh['x_lo'=2,'z'=16,'core'=2,'y'=4,'x_hi'=2] {'core','x_lo'}, dimensions={0}, use_global_device_ids=true | all-gather | bytes 655360 | tf_op jit(solution)/shard_map/all_gather | solution.py:133
  (81 shorter events, 23.5 us)
Async XLA Ops:
  0.0 6.5 %copy-start = (bf16[256,1024]{1,0:T(8,128)(2,1)S(1)}, bf16[256,1024]{1,0:T(8,128)(2,1)}, u32[]{:S(2)}) copy-start(bf16[256,1024]{1,0:T(8,128)(2,1)} %param.5) | copy-start | bytes 1572868
  0.0 22.7 %copy-start.7 = (bf16[1024,128]{1,0:T(8,128)(2,1)S(1)}, bf16[1024,128]{1,0:T(8,128)(2,1)}, u32[]{:S(2)}) copy-start(bf16[1024,128]{1,0:T(8,128)(2,1)} %param.6) | copy-start | bytes 786436
  1.0 21.7 %collective-permute-start.2 = (bf16[512,128]{1,0:T(8,128)(2,1)S(1)}, bf16[512,128]{1,0:T(8,128)(2,1)S(1)}, u32[]{:S(2)}, u32[]{:S(2)}) collective-permute-start(bf16[512,128]{1,0:T(8,128)(2,1)S(1)} %constant_dynamic-slice_fusion.1), channel_id=1, source_target_pairs={{0,1},{1,0},{2,3},{3,2},{4,5},{5,4},{6,7},{7,6},{8,9},{9,8},{10,11... | collective-permute-start | bytes 393224 | tf_op jit(solution)/shard_map/ppermute | solution.py:21
  7.6 26.8 %copy-start.5 = (bf16[256,1024]{1,0:T(8,128)(2,1)S(1)}, bf16[256,1024]{1,0:T(8,128)(2,1)}, u32[]{:S(2)}) copy-start(bf16[256,1024]{1,0:T(8,128)(2,1)} %param.4) | copy-start | bytes 1572868
  7.6 62.6 %all-to-all-start = ((bf16[16,32,1024]{2,1,0:T(8,128)(2,1)}), bf16[16,32,1024]{2,1,0:T(8,128)(2,1)S(1)}, u32[]{:S(2)}, u32[]{:S(2)}) async-start(bf16[16,32,1024]{2,1,0:T(8,128)(2,1)} %broadcast_in_dim.13), calls=%async_computation | async-start | bytes 2097152 | tf_op jit(solution)/shard_map/all_to_all | solution.py:13
  24.9 11.8 %collective-permute-start.3 = (bf16[512,256]{1,0:T(8,128)(2,1)}, bf16[512,256]{1,0:T(8,128)(2,1)S(1)}, u32[]{:S(2)}, u32[]{:S(2)}) collective-permute-start(bf16[512,256]{1,0:T(8,128)(2,1)} %pad_maximum_fusion.4), channel_id=1, source_target_pairs={{2,0},{4,2},{6,4},{0,6},{3,1},{5,3},{7,5},{1,7},{10,8},{12,10},{14... | collective-permute-start | bytes 786440 | tf_op jit(solution)/shard_map/ppermute | solution.py:26
  29.5 9.9 %collective-permute-start.4 = (bf16[512,256]{1,0:T(8,128)(2,1)}, bf16[512,256]{1,0:T(8,128)(2,1)S(1)}, u32[]{:S(2)}, u32[]{:S(2)}) collective-permute-start(bf16[512,256]{1,0:T(8,128)(2,1)} %pad_maximum_fusion.4), channel_id=1, source_target_pairs={{4,0},{6,2},{0,4},{2,6},{5,1},{7,3},{1,5},{3,7},{12,8},{14,10},{8,... | collective-permute-start | bytes 786440 | tf_op jit(solution)/shard_map/ppermute | solution.py:26
  31.8 15.1 %collective-permute-start.5 = (bf16[512,256]{1,0:T(8,128)(2,1)}, bf16[512,256]{1,0:T(8,128)(2,1)}, u32[]{:S(2)}, u32[]{:S(2)}) collective-permute-start(bf16[512,256]{1,0:T(8,128)(2,1)} %pad_maximum_fusion.4), channel_id=1, source_target_pairs={{6,0},{0,2},{2,4},{4,6},{7,1},{1,3},{3,5},{5,7},{14,8},{8,10},{10,... | collective-permute-start | bytes 786440 | tf_op jit(solution)/shard_map/ppermute | solution.py:26
  34.4 23.6 %collective-permute-start = (bf16[256,1024]{1,0:T(8,128)(2,1)S(1)}, bf16[256,1024]{1,0:T(8,128)(2,1)S(1)}, u32[]{:S(2)}, u32[]{:S(2)}) collective-permute-start(bf16[256,1024]{1,0:T(8,128)(2,1)S(1)} %copy-done.5), channel_id=1, source_target_pairs={{0,256},{256,0},{1,257},{257,1},{2,258},{258,2},{3,259},{259,3},{4... | collective-permute-start | bytes 1572872 | tf_op jit(solution)/shard_map/ppermute | solution.py:21
  53.1 7.9 %copy-start.8 = (s32[256]{0:T(256)S(1)}, s32[256]{0:T(256)}, u32[]{:S(2)}) copy-start(s32[256]{0:T(256)} %param.7) | copy-start | bytes 3076
  55.4 5.8 %collective-permute-start.6 = (bf16[512,1024]{1,0:T(8,128)(2,1)}, bf16[512,1024]{1,0:T(8,128)(2,1)}, u32[]{:S(2)}, u32[]{:S(2)}) collective-permute-start(bf16[512,1024]{1,0:T(8,128)(2,1)} %constant_dynamic-slice_fusion), channel_id=1, source_target_pairs={{0,8},{8,0},{1,9},{9,1},{2,10},{10,2},{3,11},{11,3},{4,12},{12,4},... | collective-permute-start | bytes 3145736 | tf_op jit(solution)/shard_map/ppermute | solution.py:21
  59.1 4.9 %collective-permute-start.1 = (bf16[512,1024]{1,0:T(8,128)(2,1)}, bf16[512,1024]{1,0:T(8,128)(2,1)}, u32[]{:S(2)}, u32[]{:S(2)}) collective-permute-start(bf16[512,1024]{1,0:T(8,128)(2,1)} %pad_maximum_fusion.3), channel_id=1, source_target_pairs={{0,8},{8,0},{1,9},{9,1},{2,10},{10,2},{3,11},{11,3},{4,12},{12,4},... | collective-permute-start | bytes 3145736 | tf_op jit(solution)/shard_map/ppermute | solution.py:21
  63.2 2.1 %copy-start.6 = (bf16[512,1024]{1,0:T(8,128)(2,1)}, bf16[512,1024]{1,0:T(8,128)(2,1)S(1)}, u32[]{:S(2)}) copy-start(bf16[512,1024]{1,0:T(8,128)(2,1)S(1)} %get-tuple-element.14) | copy-start | bytes 3145732
  65.2 1.3 copy-start.1
  70.2 2.6 %copy-start.9 = (bf16[1024,1024]{1,0:T(8,128)(2,1)S(1)}, bf16[1024,1024]{1,0:T(8,128)(2,1)}, u32[]{:S(2)}) copy-start(bf16[1024,1024]{1,0:T(8,128)(2,1)} %convolution_convert_fusion) | copy-start | bytes 6291460
  72.9 1.4 copy-start.10
  74.3 1.3 copy-start.3
  77.0 23.1 %all-to-all-start.2 = ((f32[16,4,128]{2,1,0:T(4,128)}), f32[16,4,128]{2,1,0:T(4,128)S(1)}, u32[]{:S(2)}, u32[]{:S(2)}) async-start(f32[16,4,128]{2,1,0:T(4,128)} %broadcast_in_dim.17), calls=%async_computation.2 | async-start | bytes 65536 | tf_op jit(solution)/shard_map/all_to_all | solution.py:13
  100.7 13.6 %all-to-all-start.1 = ((f32[32,8,128]{2,1,0:T(8,128)}), f32[32,8,128]{2,1,0:T(8,128)S(1)}, u32[]{:S(2)}, u32[]{:S(2)}) async-start(f32[32,8,128]{2,1,0:T(8,128)} %broadcast_in_dim.15), calls=%async_computation.1 | async-start | bytes 262144 | tf_op jit(solution)/shard_map/all_to_all | solution.py:13
  114.5 4.0 %copy-start.4 = (f32[512,1024]{1,0:T(8,128)S(1)}, f32[512,1024]{1,0:T(8,128)}, u32[]{:S(2)}) copy-start(f32[512,1024]{1,0:T(8,128)} %copy-done.3) | copy-start | bytes 6291460
  114.5 4.0 %copy-start.11 = (bf16[512,1024]{1,0:T(8,128)(2,1)S(1)}, bf16[512,1024]{1,0:T(8,128)(2,1)}, u32[]{:S(2)}) copy-start(bf16[512,1024]{1,0:T(8,128)(2,1)} %copy-done.10) | copy-start | bytes 3145732
  121.1 1.6 copy-start.2
  125.3 6.9 %collective-permute-start.7 = (f32[512,1024]{1,0:T(8,128)S(1)}, f32[512,1024]{1,0:T(8,128)S(1)}, u32[]{:S(2)}, u32[]{:S(2)}) collective-permute-start(f32[512,1024]{1,0:T(8,128)S(1)} %add_add_fusion), channel_id=1, source_target_pairs={{0,8},{8,0},{1,9},{9,1},{2,10},{10,2},{3,11},{11,3},{4,12},{12,4},... | collective-permute-start | bytes 6291464 | tf_op jit(solution)/shard_map/ppermute | solution.py:21

commit v2 on v1

--- a/solution.py
+++ b/solution.py
@@ -1,9 +1,12 @@
 import jax
 import jax.numpy as jnp
 from jax import lax
+from jax.experimental import pallas as pl
+from jax.experimental.pallas import tpu as pltpu
 from jax.sharding import Mesh, PartitionSpec as P
 
-DP = ("x_lo", "z", "core")
+DP = ("x_lo", "z_hi", "z_lo", "core")
+LAYERS = ("z_hi", "z_lo")
 CUTS = ("y", "x_hi")
 PLANE = ("core", "x_lo", "y", "x_hi")
 SPREAD = ("x_lo", "y", "x_hi")
@@ -33,16 +36,53 @@
     )
 
 
-def whole_projection(projection):
+def projection_strip(projection):
     half = projection.shape[0] // 2
     own = lax.dynamic_slice_in_dim(projection, lax.axis_index("core") * half, half, 0)
-    strip = in_order(own, from_twin(own, "x_hi"), "x_hi", 1)
-    turns, at = lax.axis_size("y"), lax.axis_index("y")
-    strips = [strip] + [from_ahead(strip, "y", by) for by in range(1, turns)]
-    lap = jnp.concatenate(strips + strips, 1)
-    start = (turns - at) % turns * strip.shape[1]
-    mine = lax.dynamic_slice_in_dim(lap, start, turns * strip.shape[1], 1)
-    return in_order(mine, from_twin(mine, "core"), "core", 0)
+    return in_order(own, from_twin(own, "x_hi"), "x_hi", 1)
+
+
+def projection_halves(strip):
+    strips = [strip] + [from_ahead(strip, "y", by) for by in range(1, lax.axis_size("y"))]
+    near = jnp.stack(strips)
+    return near, from_twin(near, "core")
+
+
+def project_kernel(at_ref, x_ref, near_ref, far_ref, out_ref):
+    turn, core = at_ref[0], at_ref[1]
+    turns, half, wide = near_ref.shape
+    near_x = x_ref[:, pl.ds(pl.multiple_of(core * half, half), half)]
+    far_x = x_ref[:, pl.ds(pl.multiple_of((1 - core) * half, half), half)]
+    for by in range(turns):
+        block = jnp.dot(near_x, near_ref[by], preferred_element_type=jnp.float32)
+        block += jnp.dot(far_x, far_ref[by], preferred_element_type=jnp.float32)
+        place = pl.multiple_of(lax.rem(turn + by, turns) * wide, wide)
+        out_ref[:, pl.ds(place, wide)] = block.astype(out_ref.dtype)
+
+
+def project(x, near, far):
+    rows, depth = x.shape
+    width = near.shape[0] * near.shape[2]
+    at = jnp.stack([lax.axis_index("y"), lax.axis_index("core")]).astype(jnp.int32)
+    block = 256
+    return pl.pallas_call(
+        project_kernel,
+        grid=(rows // block,),
+        out_shape=jax.ShapeDtypeStruct((rows, width), jnp.bfloat16),
+        in_specs=[
+            pl.BlockSpec(memory_space=pltpu.SMEM),
+            pl.BlockSpec((block, depth), lambda i: (i, 0)),
+            pl.BlockSpec(near.shape, lambda i: (0, 0, 0)),
+            pl.BlockSpec(far.shape, lambda i: (0, 0, 0)),
+        ],
+        out_specs=pl.BlockSpec((block, width), lambda i: (i, 0)),
+        cost_estimate=pl.CostEstimate(
+            flops=2 * rows * depth * width,
+            bytes_accessed=2 * (rows * depth + depth * width + rows * width),
+            transcendentals=0,
+        ),
+        compiler_params=pltpu.CompilerParams(vmem_limit_bytes=32 * 2**20),
+    )(at, x, near, far)
 
 
 def log_sum_exp(x, axis):
@@ -72,18 +112,20 @@
     pairs = rows * lax.axis_size(DP)
     inv_scale = width ** (-0.5)
     cut = lax.axis_index(CUTS)
-    layer = lax.axis_index("z")
     chunk = rows // cuts
 
     own = lax.dynamic_slice_in_dim(refusal_features, cut * chunk, chunk, 0)
-    refusals = from_all(own, "z").reshape(-1, depth)
-    whole = whole_projection(projection)
-    beside = from_twin(prompt_features, "x_lo")
-    pair_of_shards = jnp.concatenate([prompt_features, beside], 0)
+    refusals = from_all(own, LAYERS).reshape(-1, depth)
+
+    strip = projection_strip(projection)
+    strip, shard = lax.optimization_barrier((strip, prompt_features))
+    beside = from_twin(shard, "x_lo")
+    near, far = projection_halves(strip)
+    pair_of_shards = jnp.concatenate([shard, beside], 0)
     prompts = jnp.concatenate([pair_of_shards, from_twin(pair_of_shards, "core")], 0)
 
-    prompt_emb = jnp.dot(prompts, whole, preferred_element_type=jnp.float32).astype(jnp.bfloat16)
-    refusal_emb = jnp.dot(refusals, whole, preferred_element_type=jnp.float32).astype(jnp.bfloat16)
+    prompt_emb = project(prompts, near, far)
+    refusal_emb = project(refusals, near, far)
     scores = (
         lax.dot_general(
             refusal_emb, prompt_emb, (((1,), (1,)), ((), ())), preferred_element_type=jnp.float32
@@ -93,18 +135,27 @@
     n_keys, n_queries = scores.shape
 
     col_part = log_sum_exp(scores, 1).reshape(-1, 128)
-    col_lse = log_sum_exp(from_all(col_part, "z"), 0).reshape(n_keys)
     row_part = own_first(log_sum_exp(scores, 0).reshape(2, 2, rows)).reshape(-1, 128)
-    row_part = log_sum_exp(from_all(row_part, PLANE), 0)
-    row_lse = own_first(row_part.reshape(2, 2, rows)).reshape(n_queries)
+    col_part, row_part, scores = lax.optimization_barrier((col_part, row_part, scores))
+    cols = from_all(col_part, LAYERS)
+    cols, row_part, scores, positives = lax.optimization_barrier(
+        (cols, row_part, scores, positives)
+    )
+    all_rows = from_all(row_part, PLANE)
+    cols, all_rows, scores, positives = lax.optimization_barrier(
+        (cols, all_rows, scores, positives)
+    )
+    row_lse = own_first(log_sum_exp(all_rows, 0).reshape(2, 2, rows)).reshape(n_queries)
+    col_lse = log_sum_exp(cols, 0).reshape(n_keys)
 
     pair = jnp.concatenate([positives, jnp.full((n_queries - rows,), -1, jnp.int32)])
     key = jnp.arange(n_keys, dtype=jnp.int32)
-    place = jnp.where(key // chunk == layer, cut * chunk + key % chunk, -2)
+    place = jnp.where(key // chunk == lax.axis_index(LAYERS), cut * chunk + key % chunk, -2)
     marks = (pair[None, :] == place[:, None]).astype(jnp.float32)
     probs = jnp.exp(scores - row_lse[None, :]) + jnp.exp(scores - col_lse[:, None])
     grads = ((probs - 2.0 * marks) / (2.0 * pairs)).astype(jnp.bfloat16)
 
+    grads = lax.optimization_barrier(grads)
     prompt_grad = in_two(dot_first(grads, refusal_emb) * inv_scale)
     refusal_grad = in_two(
         jnp.dot(grads, prompt_emb, preferred_element_type=jnp.float32) * inv_scale
@@ -127,14 +178,16 @@
     pieces = kept.reshape(parts, half // parts, cuts, width // cuts).transpose(0, 2, 1, 3)
     pieces = pieces.reshape(parts * cuts, half // parts, width // cuts)
     in_layer = jnp.sum(exchange(pieces, SPREAD).astype(jnp.float32), axis=0)
-    slices = in_layer.reshape(lax.axis_size("z"), -1, width // cuts)
-    done = jnp.sum(exchange(slices, "z"), axis=0)
-    block = from_all(done, "z").reshape(in_layer.shape)
-    return lax.all_gather(block, ("core", "x_lo"), axis=0, tiled=True)
+    slices = in_layer.reshape(lax.axis_size(LAYERS), -1, width // cuts)
+    done = jnp.sum(exchange(slices, LAYERS), axis=0)
+    block = from_all(done, LAYERS).reshape(in_layer.shape)
+    return from_all(block, ("core", "x_lo")).reshape(depth, width // cuts)
 
 
 def solution(mesh):
-    split = Mesh(mesh.devices.reshape(2, 16, 2, 4, 2), ("x_lo", "z", "core", "y", "x_hi"))
+    split = Mesh(
+        mesh.devices.reshape(2, 4, 4, 2, 4, 2), ("x_lo", "z_hi", "z_lo", "core", "y", "x_hi")
+    )
     placed = (P(DP, None), P(DP, None), P(None, CUTS), P(DP))
     return jax.shard_map(
         shards, mesh=split, in_specs=placed, out_specs=P(None, CUTS), check_vma=False

time: 203 us -> 197 us (0.970)
  blocking collectives: 66.7 us -> 89.4 us
  waiting for transfers between devices: 28.4 us -> 13.6 us
  matrix products: 21.8 us -> 12.2 us
  local copies, waits for them, and re-layouts: 19.8 us -> 11.6 us
  Pallas kernels: 0 us -> 7.15 us
    all_to_all x3 -> x5, blocking collectives: 50.6 us -> 89.4 us  [exchange(): return lax.all_to_all(x, axes, split_axis=0, concat_axis=0, tiled=True)]
    all_gather x1 -> x0, blocking collectives: 16.1 us -> none  [shards(): return lax.all_gather(block, ('core', 'x_lo'), axis=0, tiled=True)]
    all_to_all x3 -> x2, waiting for transfers between devices: 18.9 us -> 10.2 us  [exchange(): return lax.all_to_all(x, axes, split_axis=0, concat_axis=0, tiled=True)]
    ppermute x3, waiting for transfers between devices: 8.67 us -> 0.89 us  [from_ahead(): lax.ppermute(x, axis, [((i + by) % devices, i) for i in range(devices)])]
    all_to_all x3 -> x2, starting transfers between devices: 32.5 us -> 24.7 us  [exchange(): return lax.all_to_all(x, axes, split_axis=0, concat_axis=0, tiled=True)]
    pallas_call x0 -> x2, Pallas kernels: none -> 7.15 us  [project(): pl.pallas_call(project_kernel, grid=(rows // block,), out_shape=jax.Shape...]
    dot_general x2 -> x0, matrix products: 6.28 us -> none  [the longest x1 3.66 us: shards(): jnp.dot(prompts, whole, preferred_element_type=jnp.float32)]
    ppermute x5, starting transfers between devices: 14.9 us -> 19.8 us  [from_twin(): return lax.ppermute(x, axis, [(0, 1), (1, 0)])]
  transfers between devices with their start and end apart: 11 -> 10, of which waited for: 5 -> 4; matrix products, arithmetic and copies ran while one was open for 13% -> 4% of each run, Pallas kernels for 0% -> 2%
where the time goes in v2:
time: 197 us; the launch traced here: 196 us
  blocking collectives  89.4 us (45%)
  starting transfers between devices  55.2 us (28%)
  waiting for transfers between devices  13.6 us (7%)
  matrix products  12.2 us (6%)
  local copies, waits for them, and re-layouts  11.6 us (6%)
  Pallas kernels  7.15 us (4%)
  other arithmetic  6.5 us (3%)
    all_to_all x5, blocking collectives, exchange(): return lax.all_to_all(x, axes, split_axis=0, concat_axis=0, tiled=True)  89.4 us
    all_to_all x2, starting transfers between devices, exchange(): return lax.all_to_all(x, axes, split_axis=0, concat_axis=0, tiled=True)  24.7 us
    ppermute x5, starting transfers between devices, from_twin(): return lax.ppermute(x, axis, [(0, 1), (1, 0)])  19.8 us
    ppermute x3, starting transfers between devices, from_ahead(): lax.ppermute(x, axis, [((i + by) % devices, i) for i in range(devices)])  10.7 us
    all_to_all x2, waiting for transfers between devices, exchange(): return lax.all_to_all(x, axes, split_axis=0, concat_axis=0, tiled=True)  10.2 us
    dot_general x9, matrix products, dot_first(): lax.dot_general(a, b, (((0,), (0,)), ((), ())), preferred_element_type=jn...  9.59 us
    unnamed x31, local copies, waits for them, and re-layouts  8.04 us
    pallas_call x2, Pallas kernels, project(): pl.pallas_call(project_kernel, grid=(rows // block,), out_shape=jax.Shape...  7.15 us
  transfers between devices with their start and end apart: 10, of which 4 were waited for; matrix products, arithmetic and copies ran while one was open for 4% of the time, Pallas kernels for 2%

profile of v2, /device:TPU:1, one launch (start us, length us, event | category | flops | bytes accessed | tf_op | source)
XLA Modules:
  0.0 196.1 jit_solution(5355822021162324532)
XLA Ops:
  2.2 15.7 %all-to-all-start = ((bf16[16,32,1024]{2,1,0:T(8,128)(2,1)}), bf16[16,32,1024]{2,1,0:T(8,128)(2,1)S(1)}, u32[]{:S(2)}, u32[]{:S(2)}) async-start(bf16[16,32,1024]{2,1,0:T(8,128)(2,1)} %broadcast_in_dim.15), calls=%async_computation | async-start | bytes 2097152 | tf_op jit(solution)/shard_map/all_to_all | solution.py:16
  17.9 4.7 %collective-permute-start = (bf16[512,128]{1,0:T(8,128)(2,1)S(1)}, bf16[512,128]{1,0:T(8,128)(2,1)S(1)}, u32[]{:S(2)}, u32[]{:S(2)}) collective-permute-start(bf16[512,128]{1,0:T(8,128)(2,1)S(1)} %constant_dynamic-slice_fusion.1), channel_id=1, source_target_pairs={{0,1},{1,0},{2,3},{3,2},{4,5},{5,4},{6,7},{7,6},{8,9},{9,8},{10,11... | collective-permute-start | bytes 393224 | tf_op jit(solution)/shard_map/ppermute | solution.py:24
  22.6 2.6 %collective-permute-done = bf16[512,128]{1,0:T(8,128)(2,1)S(1)} collective-permute-done((bf16[512,128]{1,0:T(8,128)(2,1)S(1)}, bf16[512,128]{1,0:T(8,128)(2,1)S(1)}, u32[]{:S(2)}, u32[]{:S(2)}) %collective-permute-start) | collective-permute-done | bytes 131104 | tf_op jit(solution)/shard_map/ppermute | solution.py:24
  25.3 3.1 %collective-permute-start.1 = (bf16[256,1024]{1,0:T(8,128)(2,1)S(1)}, bf16[256,1024]{1,0:T(8,128)(2,1)S(1)}, u32[]{:S(2)}, u32[]{:S(2)}) collective-permute-start(bf16[256,1024]{1,0:T(8,128)(2,1)S(1)} %copy-done.9), channel_id=1, source_target_pairs={{0,256},{256,0},{1,257},{257,1},{2,258},{258,2},{3,259},{259,3},{4... | collective-permute-start | bytes 1572872 | tf_op jit(solution)/shard_map/ppermute | solution.py:24
  28.4 3.2 %collective-permute-start.5 = (bf16[512,256]{1,0:T(8,128)(2,1)S(1)}, bf16[512,256]{1,0:T(8,128)(2,1)S(1)}, u32[]{:S(2)}, u32[]{:S(2)}) collective-permute-start(bf16[512,256]{1,0:T(8,128)(2,1)S(1)} %pad_maximum_fusion.2), channel_id=1, source_target_pairs={{6,0},{0,2},{2,4},{4,6},{7,1},{1,3},{3,5},{5,7},{14,8},{8,10},{10,... | collective-permute-start | bytes 786440 | tf_op jit(solution)/shard_map/ppermute | solution.py:29
  31.6 4.5 %collective-permute-start.4 = (bf16[512,256]{1,0:T(8,128)(2,1)S(1)}, bf16[512,256]{1,0:T(8,128)(2,1)S(1)}, u32[]{:S(2)}, u32[]{:S(2)}) collective-permute-start(bf16[512,256]{1,0:T(8,128)(2,1)S(1)} %pad_maximum_fusion.2), channel_id=1, source_target_pairs={{4,0},{6,2},{0,4},{2,6},{5,1},{7,3},{1,5},{3,7},{12,8},{14,10},{8,... | collective-permute-start | bytes 786440 | tf_op jit(solution)/shard_map/ppermute | solution.py:29
  36.2 3.0 %collective-permute-start.3 = (bf16[512,256]{1,0:T(8,128)(2,1)S(1)}, bf16[512,256]{1,0:T(8,128)(2,1)S(1)}, u32[]{:S(2)}, u32[]{:S(2)}) collective-permute-start(bf16[512,256]{1,0:T(8,128)(2,1)S(1)} %pad_maximum_fusion.2), channel_id=1, source_target_pairs={{2,0},{4,2},{6,4},{0,6},{3,1},{5,3},{7,5},{1,7},{10,8},{12,10},{14... | collective-permute-start | bytes 786440 | tf_op jit(solution)/shard_map/ppermute | solution.py:29
  40.3 5.1 %collective-permute-start.2 = (bf16[512,1024]{1,0:T(8,128)(2,1)}, bf16[512,1024]{1,0:T(8,128)(2,1)}, u32[]{:S(2)}, u32[]{:S(2)}) collective-permute-start(bf16[512,1024]{1,0:T(8,128)(2,1)} %pad_maximum_fusion), channel_id=1, source_target_pairs={{0,8},{8,0},{1,9},{9,1},{2,10},{10,2},{3,11},{11,3},{4,12},{12,4},... | collective-permute-start | bytes 3145736 | tf_op jit(solution)/shard_map/ppermute | solution.py:24
  46.5 4.2 %collective-permute-start.6 = (bf16[4,512,256]{2,1,0:T(8,128)(2,1)S(1)}, bf16[4,512,256]{2,1,0:T(8,128)(2,1)}, u32[]{:S(2)}, u32[]{:S(2)}) collective-permute-start(bf16[4,512,256]{2,1,0:T(8,128)(2,1)S(1)} %pad_maximum_fusion.1.near_ref), channel_id=1, source_target_pairs={{0,8},{8,0},{1,9},{9,1},{2,10},{10,2},{3,11},{11,3},{4,12},{12,4},... | collective-permute-start | bytes 3145736 | tf_op jit(solution)/shard_map/ppermute | solution.py:24
  51.9 1.3 constant_dynamic-update-slice_fusion.x_ref
  53.2 4.3 %shard_map.47 = bf16[1024,1024]{1,0:T(8,128)(2,1)S(1)} custom-call(s32[2]{0:T(128)S(1)} %pad_add_fusion.at_ref, bf16[1024,1024]{1,0:T(8,128)(2,1)S(1)} %constant_dynamic-update-slice_fusion.x_ref, bf16[4,512,256]{2,1,0:T(8,128)(2,1)S(1)} %pad_maximum_fusion.1.near_ref, bf16[4,512,256]{2,1,0:T(8,128)(2,1)} %collective-permute-done.6.far_ref), custom_call_target="tpu_custom_call" | custom-call | flops 2147483648 | bytes 6291456 | tf_op jit(solution)/shard_map/pallas_call | solution.py:68
  57.5 1.3 copy-done.1
  58.9 1.3 copy-done.5
  60.2 2.6 %all-to-all-done = bf16[16,32,1024]{2,1,0:T(8,128)(2,1)S(1)} async-done(((bf16[16,32,1024]{2,1,0:T(8,128)(2,1)}), bf16[16,32,1024]{2,1,0:T(8,128)(2,1)S(1)}, u32[]{:S(2)}, u32[]{:S(2)}) %all-to-all-start) | async-done | bytes 1048608 | tf_op jit(solution)/shard_map/all_to_all | solution.py:16
  62.8 2.9 %shard_map.46 = bf16[512,1024]{1,0:T(8,128)(2,1)S(1)} custom-call(s32[2]{0:T(128)S(1)} %pad_add_fusion.at_ref, bf16[512,1024]{1,0:T(8,128)(2,1)S(1)} %bitcast.30, bf16[4,512,256]{2,1,0:T(8,128)(2,1)S(1)} %pad_maximum_fusion.1.near_ref, bf16[4,512,256]{2,1,0:T(8,128)(2,1)} %collective-permute-done.6.far_ref), custom_call_target="tpu_custom_call" | custom-call | flops 1073741824 | bytes 4194304 | tf_op jit(solution)/shard_map/pallas_call | solution.py:68
  65.7 1.4 fusion.48
  67.1 1.3 copy-done.8
  69.3 24.5 %all_to_all.35 = f32[16,4,128]{2,1,0:T(4,128)S(1)} all-to-all(f32[16,4,128]{2,1,0:T(4,128)S(1)} %broadcast_in_dim.16), channel_id=1, replica_groups=mesh['x_lo'=2,'z_hi'=4,'z_lo'=4,'core'=2,'y'=4,'x_hi'=2] {'z_hi','z_lo'}, dimensions={0} | all-to-all | bytes 65536 | tf_op jit(solution)/shard_map/all_to_all | solution.py:16
  94.5 9.0 %all-to-all-start.2 = ((f32[32,8,128]{2,1,0:T(8,128)}), f32[32,8,128]{2,1,0:T(8,128)S(1)}, u32[]{:S(2)}, u32[]{:S(2)}) async-start(f32[32,8,128]{2,1,0:T(8,128)} %broadcast_in_dim.17), calls=%async_computation.2 | async-start | bytes 262144 | tf_op jit(solution)/shard_map/all_to_all | solution.py:16
  103.5 7.6 %all-to-all-done.2 = f32[32,8,128]{2,1,0:T(8,128)S(1)} async-done(((f32[32,8,128]{2,1,0:T(8,128)}), f32[32,8,128]{2,1,0:T(8,128)S(1)}, u32[]{:S(2)}, u32[]{:S(2)}) %all-to-all-start.2) | async-done | bytes 131104 | tf_op jit(solution)/shard_map/all_to_all | solution.py:16
  111.4 2.6 %multiply_convert_fusion = bf16[512,1024]{1,0:T(8,128)(2,1)S(1)} fusion(f32[512,1024]{1,0:T(8,128)} %copy-done.8, s32[1024]{0:T(1024)S(1)} %concatenate.16, f32[512]{0:T(512)S(1)} %add_bitcast_fusion, f32[1024]{0:T(1024)S(1)} %bitcast.44, s32[512]{0:T(512)S(1)} %fusion.28), kind=kLoop, calls=%fused_computation.9 | loop fusion | flops 4194304 | bytes 3158016 | tf_op jit(solution)/shard_map/convert_element_type | solution.py:156
  114.0 1.3 fusion.50
  115.3 1.3 fusion.49
  119.0 1.3 fusion.4
  120.2 1.3 add_add_fusion
  121.5 2.6 %collective-permute-start.7 = (f32[512,1024]{1,0:T(8,128)S(1)}, f32[512,1024]{1,0:T(8,128)S(1)}, u32[]{:S(2)}, u32[]{:S(2)}) collective-permute-start(f32[512,1024]{1,0:T(8,128)S(1)} %add_add_fusion), channel_id=1, source_target_pairs={{0,8},{8,0},{1,9},{9,1},{2,10},{10,2},{3,11},{11,3},{4,12},{12,4},... | collective-permute-start | bytes 6291464 | tf_op jit(solution)/shard_map/ppermute | solution.py:24
  125.8 1.3 fusion.8
  127.1 1.3 fusion.6
  130.2 18.9 %all_to_all.36 = bf16[16,256,128]{2,1,0:T(8,128)(2,1)S(1)} all-to-all(bf16[16,256,128]{2,1,0:T(8,128)(2,1)S(1)} %bitcast.36), channel_id=1, replica_groups=mesh['x_lo'=2,'z_hi'=4,'z_lo'=4,'core'=2,'y'=4,'x_hi'=2] {'x_lo','y','x_..., dimensions={0} | all-to-all | bytes 2097152 | tf_op jit(solution)/shard_map/all_to_all | solution.py:16
  149.2 14.5 %all_to_all.37 = f32[16,16,128]{2,1,0:T(8,128)S(1)} all-to-all(f32[16,16,128]{2,1,0:T(8,128)S(1)} %bitcast.39), channel_id=1, replica_groups=mesh['x_lo'=2,'z_hi'=4,'z_lo'=4,'core'=2,'y'=4,'x_hi'=2] {'z_hi','z_lo'}, dimensions={0} | all-to-all | bytes 262144 | tf_op jit(solution)/shard_map/all_to_all | solution.py:16
  163.8 17.1 %all_to_all.38 = f32[16,16,128]{2,1,0:T(8,128)S(1)} all-to-all(f32[16,16,128]{2,1,0:T(8,128)S(1)} %broadcast_in_dim.20), channel_id=1, replica_groups=mesh['x_lo'=2,'z_hi'=4,'z_lo'=4,'core'=2,'y'=4,'x_hi'=2] {'z_hi','z_lo'}, dimensions={0} | all-to-all | bytes 262144 | tf_op jit(solution)/shard_map/all_to_all | solution.py:16
  181.0 14.3 %all_to_all.39 = f32[4,256,128]{2,1,0:T(8,128)S(1)} all-to-all(f32[4,256,128]{2,1,0:T(8,128)S(1)} %broadcast_in_dim.22), channel_id=1, replica_groups=mesh['x_lo'=2,'z_hi'=4,'z_lo'=4,'core'=2,'y'=4,'x_hi'=2] {'core','x_lo'}, dimensions={0} | all-to-all | bytes 1048576 | tf_op jit(solution)/shard_map/all_to_all | solution.py:16
  (75 shorter events, 14.1 us)
Async XLA Ops:
  0.0 1.0 copy-start
  0.0 17.9 %copy-start.11 = (bf16[1024,128]{1,0:T(8,128)(2,1)S(1)}, bf16[1024,128]{1,0:T(8,128)(2,1)}, u32[]{:S(2)}) copy-start(bf16[1024,128]{1,0:T(8,128)(2,1)} %param.6) | copy-start | bytes 786436
  1.0 24.2 %copy-start.9 = (bf16[256,1024]{1,0:T(8,128)(2,1)S(1)}, bf16[256,1024]{1,0:T(8,128)(2,1)}, u32[]{:S(2)}) copy-start(bf16[256,1024]{1,0:T(8,128)(2,1)} %param.4) | copy-start | bytes 1572868
  2.2 60.6 %all-to-all-start = ((bf16[16,32,1024]{2,1,0:T(8,128)(2,1)}), bf16[16,32,1024]{2,1,0:T(8,128)(2,1)S(1)}, u32[]{:S(2)}, u32[]{:S(2)}) async-start(bf16[16,32,1024]{2,1,0:T(8,128)(2,1)} %broadcast_in_dim.15), calls=%async_computation | async-start | bytes 2097152 | tf_op jit(solution)/shard_map/all_to_all | solution.py:16
  17.9 7.2 %collective-permute-start = (bf16[512,128]{1,0:T(8,128)(2,1)S(1)}, bf16[512,128]{1,0:T(8,128)(2,1)S(1)}, u32[]{:S(2)}, u32[]{:S(2)}) collective-permute-start(bf16[512,128]{1,0:T(8,128)(2,1)S(1)} %constant_dynamic-slice_fusion.1), channel_id=1, source_target_pairs={{0,1},{1,0},{2,3},{3,2},{4,5},{5,4},{6,7},{7,6},{8,9},{9,8},{10,11... | collective-permute-start | bytes 393224 | tf_op jit(solution)/shard_map/ppermute | solution.py:24
  25.3 13.9 %collective-permute-start.1 = (bf16[256,1024]{1,0:T(8,128)(2,1)S(1)}, bf16[256,1024]{1,0:T(8,128)(2,1)S(1)}, u32[]{:S(2)}, u32[]{:S(2)}) collective-permute-start(bf16[256,1024]{1,0:T(8,128)(2,1)S(1)} %copy-done.9), channel_id=1, source_target_pairs={{0,256},{256,0},{1,257},{257,1},{2,258},{258,2},{3,259},{259,3},{4... | collective-permute-start | bytes 1572872 | tf_op jit(solution)/shard_map/ppermute | solution.py:24
  28.4 17.1 %collective-permute-start.5 = (bf16[512,256]{1,0:T(8,128)(2,1)S(1)}, bf16[512,256]{1,0:T(8,128)(2,1)S(1)}, u32[]{:S(2)}, u32[]{:S(2)}) collective-permute-start(bf16[512,256]{1,0:T(8,128)(2,1)S(1)} %pad_maximum_fusion.2), channel_id=1, source_target_pairs={{6,0},{0,2},{2,4},{4,6},{7,1},{1,3},{3,5},{5,7},{14,8},{8,10},{10,... | collective-permute-start | bytes 786440 | tf_op jit(solution)/shard_map/ppermute | solution.py:29
  31.6 13.9 %collective-permute-start.4 = (bf16[512,256]{1,0:T(8,128)(2,1)S(1)}, bf16[512,256]{1,0:T(8,128)(2,1)S(1)}, u32[]{:S(2)}, u32[]{:S(2)}) collective-permute-start(bf16[512,256]{1,0:T(8,128)(2,1)S(1)} %pad_maximum_fusion.2), channel_id=1, source_target_pairs={{4,0},{6,2},{0,4},{2,6},{5,1},{7,3},{1,5},{3,7},{12,8},{14,10},{8,... | collective-permute-start | bytes 786440 | tf_op jit(solution)/shard_map/ppermute | solution.py:29
  36.2 10.2 %collective-permute-start.3 = (bf16[512,256]{1,0:T(8,128)(2,1)S(1)}, bf16[512,256]{1,0:T(8,128)(2,1)S(1)}, u32[]{:S(2)}, u32[]{:S(2)}) collective-permute-start(bf16[512,256]{1,0:T(8,128)(2,1)S(1)} %pad_maximum_fusion.2), channel_id=1, source_target_pairs={{2,0},{4,2},{6,4},{0,6},{3,1},{5,3},{7,5},{1,7},{10,8},{12,10},{14... | collective-permute-start | bytes 786440 | tf_op jit(solution)/shard_map/ppermute | solution.py:29
  39.1 7.3 %copy-start.10 = (bf16[256,1024]{1,0:T(8,128)(2,1)}, bf16[256,1024]{1,0:T(8,128)(2,1)S(1)}, u32[]{:S(2)}) copy-start(bf16[256,1024]{1,0:T(8,128)(2,1)S(1)} %collective-permute-done.1) | copy-start | bytes 1572868
  40.3 11.6 %collective-permute-start.2 = (bf16[512,1024]{1,0:T(8,128)(2,1)}, bf16[512,1024]{1,0:T(8,128)(2,1)}, u32[]{:S(2)}, u32[]{:S(2)}) collective-permute-start(bf16[512,1024]{1,0:T(8,128)(2,1)} %pad_maximum_fusion), channel_id=1, source_target_pairs={{0,8},{8,0},{1,9},{9,1},{2,10},{10,2},{3,11},{11,3},{4,12},{12,4},... | collective-permute-start | bytes 3145736 | tf_op jit(solution)/shard_map/ppermute | solution.py:24
  46.5 6.7 %collective-permute-start.6 = (bf16[4,512,256]{2,1,0:T(8,128)(2,1)S(1)}, bf16[4,512,256]{2,1,0:T(8,128)(2,1)}, u32[]{:S(2)}, u32[]{:S(2)}) collective-permute-start(bf16[4,512,256]{2,1,0:T(8,128)(2,1)S(1)} %pad_maximum_fusion.1.near_ref), channel_id=1, source_target_pairs={{0,8},{8,0},{1,9},{9,1},{2,10},{10,2},{3,11},{11,3},{4,12},{12,4},... | collective-permute-start | bytes 3145736 | tf_op jit(solution)/shard_map/ppermute | solution.py:24
  57.5 1.4 copy-start.1
  58.9 1.3 copy-start.5
  62.8 2.9 %copy-start.6 = (bf16[1024,1024]{1,0:T(8,128)(2,1)S(1)}, bf16[1024,1024]{1,0:T(8,128)(2,1)}, u32[]{:S(2)}) copy-start(bf16[1024,1024]{1,0:T(8,128)(2,1)} %copy-done.5) | copy-start | bytes 6291460
  65.7 1.4 copy-start.3
  67.0 1.3 copy-start.8
  67.1 44.3 %copy-start.12 = (s32[256]{0:T(256)S(1)}, s32[256]{0:T(256)}, u32[]{:S(2)}) copy-start(s32[256]{0:T(256)} %param.7) | copy-start | bytes 3076
  94.5 16.6 %all-to-all-start.2 = ((f32[32,8,128]{2,1,0:T(8,128)}), f32[32,8,128]{2,1,0:T(8,128)S(1)}, u32[]{:S(2)}, u32[]{:S(2)}) async-start(f32[32,8,128]{2,1,0:T(8,128)} %broadcast_in_dim.17), calls=%async_computation.2 | async-start | bytes 262144 | tf_op jit(solution)/shard_map/all_to_all | solution.py:16
  111.3 2.7 %copy-start.7 = (bf16[1024,1024]{1,0:T(8,128)(2,1)S(1)}, bf16[1024,1024]{1,0:T(8,128)(2,1)}, u32[]{:S(2)}) copy-start(bf16[1024,1024]{1,0:T(8,128)(2,1)} %copy-done.5) | copy-start | bytes 6291460
  114.0 1.3 copy-start.4
  117.4 1.6 copy-start.2
  121.5 6.9 %collective-permute-start.7 = (f32[512,1024]{1,0:T(8,128)S(1)}, f32[512,1024]{1,0:T(8,128)S(1)}, u32[]{:S(2)}, u32[]{:S(2)}) collective-permute-start(f32[512,1024]{1,0:T(8,128)S(1)} %add_add_fusion), channel_id=1, source_target_pairs={{0,8},{8,0},{1,9},{9,1},{2,10},{10,2},{3,11},{11,3},{4,12},{12,4},... | collective-permute-start | bytes 6291464 | tf_op jit(solution)/shard_map/ppermute | solution.py:24

commit v3 on v2

--- a/solution.py
+++ b/solution.py
@@ -81,7 +81,7 @@
             bytes_accessed=2 * (rows * depth + depth * width + rows * width),
             transcendentals=0,
         ),
-        compiler_params=pltpu.CompilerParams(vmem_limit_bytes=32 * 2**20),
+        compiler_params=pltpu.CompilerParams(vmem_limit_bytes=12 * 2**20),
     )(at, x, near, far)
 
 
@@ -105,6 +105,12 @@
     return lax.dot_general(a, b, (((0,), (0,)), ((), ())), preferred_element_type=jnp.float32)
 
 
+def score(refusal_emb, prompt_emb, inv_scale):
+    return inv_scale * lax.dot_general(
+        refusal_emb, prompt_emb, (((1,), (1,)), ((), ())), preferred_element_type=jnp.float32
+    )
+
+
 def shards(prompt_features, refusal_features, projection, positives):
     rows, depth = prompt_features.shape
     cuts = lax.axis_size(CUTS)
@@ -126,24 +132,17 @@
 
     prompt_emb = project(prompts, near, far)
     refusal_emb = project(refusals, near, far)
-    scores = (
-        lax.dot_general(
-            refusal_emb, prompt_emb, (((1,), (1,)), ((), ())), preferred_element_type=jnp.float32
-        )
-        * inv_scale
-    )
+    scores = score(refusal_emb, prompt_emb, inv_scale)
     n_keys, n_queries = scores.shape
 
     col_part = log_sum_exp(scores, 1).reshape(-1, 128)
     row_part = own_first(log_sum_exp(scores, 0).reshape(2, 2, rows)).reshape(-1, 128)
-    col_part, row_part, scores = lax.optimization_barrier((col_part, row_part, scores))
+    col_part, row_part = lax.optimization_barrier((col_part, row_part))
     cols = from_all(col_part, LAYERS)
-    cols, row_part, scores, positives = lax.optimization_barrier(
-        (cols, row_part, scores, positives)
-    )
+    cols, row_part, positives = lax.optimization_barrier((cols, row_part, positives))
     all_rows = from_all(row_part, PLANE)
-    cols, all_rows, scores, positives = lax.optimization_barrier(
-        (cols, all_rows, scores, positives)
+    cols, all_rows, positives, refusal_emb = lax.optimization_barrier(
+        (cols, all_rows, positives, refusal_emb)
     )
     row_lse = own_first(log_sum_exp(all_rows, 0).reshape(2, 2, rows)).reshape(n_queries)
     col_lse = log_sum_exp(cols, 0).reshape(n_keys)
@@ -152,22 +151,23 @@
     key = jnp.arange(n_keys, dtype=jnp.int32)
     place = jnp.where(key // chunk == lax.axis_index(LAYERS), cut * chunk + key % chunk, -2)
     marks = (pair[None, :] == place[:, None]).astype(jnp.float32)
+    scores = score(refusal_emb, prompt_emb, inv_scale)
     probs = jnp.exp(scores - row_lse[None, :]) + jnp.exp(scores - col_lse[:, None])
     grads = ((probs - 2.0 * marks) / (2.0 * pairs)).astype(jnp.bfloat16)
+    grads = lax.optimization_barrier(grads)
 
-    grads = lax.optimization_barrier(grads)
-    prompt_grad = in_two(dot_first(grads, refusal_emb) * inv_scale)
+    prompt_sum = in_two(jnp.dot(grads, prompts, preferred_element_type=jnp.float32) * inv_scale)
     refusal_grad = in_two(
         jnp.dot(grads, prompt_emb, preferred_element_type=jnp.float32) * inv_scale
     )
 
     def product(start, count):
-        left = lax.dynamic_slice_in_dim(prompts, start, count, 1)
         right = lax.dynamic_slice_in_dim(refusals, start, count, 1)
+        left = [lax.dynamic_slice_in_dim(x, start, count, 1) for x in prompt_sum]
         return (
-            dot_first(left, prompt_grad[0])
+            dot_first(left[0], refusal_emb)
             + dot_first(right, refusal_grad[0])
-            + (dot_first(left, prompt_grad[1]) + dot_first(right, refusal_grad[1]))
+            + (dot_first(left[1], refusal_emb) + dot_first(right, refusal_grad[1]))
         )
 
     core = lax.axis_index("core")

time: 197 us -> 194 us (0.985)
  other arithmetic: 6.5 us -> 2.7 us
    dot_general x1 -> x3, matrix products: 1.37 us -> 6.26 us  [the longest x2 4.99 us: score(): lax.dot_general(refusal_emb, prompt_emb, (((1,), (1,)), ((), ())), prefer...]
    dot_general x9 -> x8, matrix products: 9.59 us -> 6.28 us  [dot_first(): lax.dot_general(a, b, (((0,), (0,)), ((), ())), preferred_element_type=jn...]
    convert_element_type x1 -> x0, other arithmetic: 2.64 us -> none  [shards(): grads = ((probs - 2.0 * marks) / (2.0 * pairs)).astype(jnp.bfloat16)]
    unnamed x31 -> x29, local copies, waits for them, and re-layouts: 8.04 us -> 7.43 us
  transfers between devices with their start and end apart: 10 -> 10, of which waited for: 4 -> 5; matrix products, arithmetic and copies ran while one was open for 4% -> 3% of each run, Pallas kernels for 2% -> 2%
where the time goes in v3:
time: 194 us; the launch traced here: 193 us
  blocking collectives  88 us (45%)
  starting transfers between devices  54.9 us (28%)
  waiting for transfers between devices  14.9 us (8%)
  matrix products  13.8 us (7%)
  local copies, waits for them, and re-layouts  11 us (6%)
  Pallas kernels  7.14 us (4%)
  other arithmetic  2.7 us (1%)
    all_to_all x5, blocking collectives, exchange(): return lax.all_to_all(x, axes, split_axis=0, concat_axis=0, tiled=True)  88 us
    all_to_all x2, starting transfers between devices, exchange(): return lax.all_to_all(x, axes, split_axis=0, concat_axis=0, tiled=True)  24.7 us
    ppermute x5, starting transfers between devices, from_twin(): return lax.ppermute(x, axis, [(0, 1), (1, 0)])  19.5 us
    ppermute x3, starting transfers between devices, from_ahead(): lax.ppermute(x, axis, [((i + by) % devices, i) for i in range(devices)])  10.7 us
    all_to_all x2, waiting for transfers between devices, exchange(): return lax.all_to_all(x, axes, split_axis=0, concat_axis=0, tiled=True)  10.1 us
    unnamed x29, local copies, waits for them, and re-layouts  7.43 us
    pallas_call x2, Pallas kernels, project(): pl.pallas_call(project_kernel, grid=(rows // block,), out_shape=jax.Shape...  7.14 us
    dot_general x8, matrix products, dot_first(): lax.dot_general(a, b, (((0,), (0,)), ((), ())), preferred_element_type=jn...  6.28 us
  transfers between devices with their start and end apart: 10, of which 5 were waited for; matrix products, arithmetic and copies ran while one was open for 3% of the time, Pallas kernels for 2%

profile of v3, /device:TPU:1, one launch (start us, length us, event | category | flops | bytes accessed | tf_op | source)
XLA Modules:
  0.0 192.9 jit_solution(3611123348980917167)
XLA Ops:
  1.1 1.1 broadcast_in_dim.15
  2.2 15.7 %all-to-all-start = ((bf16[16,32,1024]{2,1,0:T(8,128)(2,1)}), bf16[16,32,1024]{2,1,0:T(8,128)(2,1)S(1)}, u32[]{:S(2)}, u32[]{:S(2)}) async-start(bf16[16,32,1024]{2,1,0:T(8,128)(2,1)} %broadcast_in_dim.15), calls=%async_computation | async-start | bytes 2097152 | tf_op jit(solution)/shard_map/all_to_all | solution.py:16
  17.9 4.7 %collective-permute-start = (bf16[512,128]{1,0:T(8,128)(2,1)S(1)}, bf16[512,128]{1,0:T(8,128)(2,1)S(1)}, u32[]{:S(2)}, u32[]{:S(2)}) collective-permute-start(bf16[512,128]{1,0:T(8,128)(2,1)S(1)} %constant_dynamic-slice_fusion), channel_id=1, source_target_pairs={{0,1},{1,0},{2,3},{3,2},{4,5},{5,4},{6,7},{7,6},{8,9},{9,8},{10,11... | collective-permute-start | bytes 393224 | tf_op jit(solution)/shard_map/ppermute | solution.py:24
  22.6 2.6 %collective-permute-done = bf16[512,128]{1,0:T(8,128)(2,1)S(1)} collective-permute-done((bf16[512,128]{1,0:T(8,128)(2,1)S(1)}, bf16[512,128]{1,0:T(8,128)(2,1)S(1)}, u32[]{:S(2)}, u32[]{:S(2)}) %collective-permute-start) | collective-permute-done | bytes 131104 | tf_op jit(solution)/shard_map/ppermute | solution.py:24
  25.3 3.1 %collective-permute-start.5 = (bf16[256,1024]{1,0:T(8,128)(2,1)S(1)}, bf16[256,1024]{1,0:T(8,128)(2,1)S(1)}, u32[]{:S(2)}, u32[]{:S(2)}) collective-permute-start(bf16[256,1024]{1,0:T(8,128)(2,1)S(1)} %copy-done.8), channel_id=1, source_target_pairs={{0,256},{256,0},{1,257},{257,1},{2,258},{258,2},{3,259},{259,3},{4... | collective-permute-start | bytes 1572872 | tf_op jit(solution)/shard_map/ppermute | solution.py:24
  28.4 3.2 %collective-permute-start.3 = (bf16[512,256]{1,0:T(8,128)(2,1)S(1)}, bf16[512,256]{1,0:T(8,128)(2,1)S(1)}, u32[]{:S(2)}, u32[]{:S(2)}) collective-permute-start(bf16[512,256]{1,0:T(8,128)(2,1)S(1)} %pad_maximum_fusion.2), channel_id=1, source_target_pairs={{6,0},{0,2},{2,4},{4,6},{7,1},{1,3},{3,5},{5,7},{14,8},{8,10},{10,... | collective-permute-start | bytes 786440 | tf_op jit(solution)/shard_map/ppermute | solution.py:29
  31.6 4.5 %collective-permute-start.2 = (bf16[512,256]{1,0:T(8,128)(2,1)S(1)}, bf16[512,256]{1,0:T(8,128)(2,1)S(1)}, u32[]{:S(2)}, u32[]{:S(2)}) collective-permute-start(bf16[512,256]{1,0:T(8,128)(2,1)S(1)} %pad_maximum_fusion.2), channel_id=1, source_target_pairs={{4,0},{6,2},{0,4},{2,6},{5,1},{7,3},{1,5},{3,7},{12,8},{14,10},{8,... | collective-permute-start | bytes 786440 | tf_op jit(solution)/shard_map/ppermute | solution.py:29
  36.2 3.0 %collective-permute-start.1 = (bf16[512,256]{1,0:T(8,128)(2,1)S(1)}, bf16[512,256]{1,0:T(8,128)(2,1)S(1)}, u32[]{:S(2)}, u32[]{:S(2)}) collective-permute-start(bf16[512,256]{1,0:T(8,128)(2,1)S(1)} %pad_maximum_fusion.2), channel_id=1, source_target_pairs={{2,0},{4,2},{6,4},{0,6},{3,1},{5,3},{7,5},{1,7},{10,8},{12,10},{14... | collective-permute-start | bytes 786440 | tf_op jit(solution)/shard_map/ppermute | solution.py:29
  39.2 1.2 pad_maximum_fusion.1
  40.3 5.1 %collective-permute-start.6 = (bf16[512,1024]{1,0:T(8,128)(2,1)}, bf16[512,1024]{1,0:T(8,128)(2,1)}, u32[]{:S(2)}, u32[]{:S(2)}) collective-permute-start(bf16[512,1024]{1,0:T(8,128)(2,1)} %pad_maximum_fusion.1), channel_id=1, source_target_pairs={{0,8},{8,0},{1,9},{9,1},{2,10},{10,2},{3,11},{11,3},{4,12},{12,4},... | collective-permute-start | bytes 3145736 | tf_op jit(solution)/shard_map/ppermute | solution.py:24
  46.5 4.2 %collective-permute-start.4 = (bf16[4,512,256]{2,1,0:T(8,128)(2,1)S(1)}, bf16[4,512,256]{2,1,0:T(8,128)(2,1)}, u32[]{:S(2)}, u32[]{:S(2)}) collective-permute-start(bf16[4,512,256]{2,1,0:T(8,128)(2,1)S(1)} %pad_maximum_fusion.near_ref), channel_id=1, source_target_pairs={{0,8},{8,0},{1,9},{9,1},{2,10},{10,2},{3,11},{11,3},{4,12},{12,4},... | collective-permute-start | bytes 3145736 | tf_op jit(solution)/shard_map/ppermute | solution.py:24
  50.9 1.1 constant_dynamic-update-slice_fusion.1
  51.9 1.3 constant_dynamic-update-slice_fusion.x_ref
  53.3 4.3 %shard_map.47 = bf16[1024,1024]{1,0:T(8,128)(2,1)S(1)} custom-call(s32[2]{0:T(128)S(1)} %pad_add_fusion.at_ref, bf16[1024,1024]{1,0:T(8,128)(2,1)S(1)} %constant_dynamic-update-slice_fusion.x_ref, bf16[4,512,256]{2,1,0:T(8,128)(2,1)S(1)} %pad_maximum_fusion.near_ref, bf16[4,512,256]{2,1,0:T(8,128)(2,1)} %collective-permute-done.4.far_ref), custom_call_target="tpu_custom_call" | custom-call | flops 2147483648 | bytes 6291456 | tf_op jit(solution)/shard_map/pallas_call | solution.py:68
  57.5 1.3 copy-done.3
  58.9 1.3 copy-done.5
  60.2 2.6 %all-to-all-done = bf16[16,32,1024]{2,1,0:T(8,128)(2,1)S(1)} async-done(((bf16[16,32,1024]{2,1,0:T(8,128)(2,1)}), bf16[16,32,1024]{2,1,0:T(8,128)(2,1)S(1)}, u32[]{:S(2)}, u32[]{:S(2)}) %all-to-all-start) | async-done | bytes 1048608 | tf_op jit(solution)/shard_map/all_to_all | solution.py:16
  62.8 1.2 copy-done.2
  64.0 2.9 %shard_map.46 = bf16[512,1024]{1,0:T(8,128)(2,1)S(1)} custom-call(s32[2]{0:T(128)S(1)} %pad_add_fusion.at_ref, bf16[512,1024]{1,0:T(8,128)(2,1)S(1)} %bitcast.36, bf16[4,512,256]{2,1,0:T(8,128)(2,1)S(1)} %copy-done.2, bf16[4,512,256]{2,1,0:T(8,128)(2,1)} %collective-permute-done.4.far_ref), custom_call_target="tpu_custom_call" | custom-call | flops 1073741824 | bytes 4194304 | tf_op jit(solution)/shard_map/pallas_call | solution.py:68
  66.9 1.4 multiply_reduce_fusion
  69.3 24.5 %all_to_all.35 = f32[16,4,128]{2,1,0:T(4,128)S(1)} all-to-all(f32[16,4,128]{2,1,0:T(4,128)S(1)} %broadcast_in_dim.16), channel_id=1, replica_groups=mesh['x_lo'=2,'z_hi'=4,'z_lo'=4,'core'=2,'y'=4,'x_hi'=2] {'z_hi','z_lo'}, dimensions={0} | all-to-all | bytes 65536 | tf_op jit(solution)/shard_map/all_to_all | solution.py:16
  94.4 9.0 %all-to-all-start.2 = ((f32[32,8,128]{2,1,0:T(8,128)}), f32[32,8,128]{2,1,0:T(8,128)S(1)}, u32[]{:S(2)}, u32[]{:S(2)}) async-start(f32[32,8,128]{2,1,0:T(8,128)} %broadcast_in_dim.17), calls=%async_computation.2 | async-start | bytes 262144 | tf_op jit(solution)/shard_map/all_to_all | solution.py:16
  103.4 7.6 %all-to-all-done.2 = f32[32,8,128]{2,1,0:T(8,128)S(1)} async-done(((f32[32,8,128]{2,1,0:T(8,128)}), f32[32,8,128]{2,1,0:T(8,128)S(1)}, u32[]{:S(2)}, u32[]{:S(2)}) %all-to-all-start.2) | async-done | bytes 131104 | tf_op jit(solution)/shard_map/all_to_all | solution.py:16
  111.3 3.6 %multiply_convert_fusion = bf16[512,1024]{1,0:T(8,128)(2,1)S(1)} fusion(bf16[512,1024]{1,0:T(8,128)(2,1)S(1)} %shard_map.46, bf16[1024,1024]{1,0:T(8,128)(2,1)} %copy-done.5, s32[1024]{0:T(1024)S(1)} %concatenate.16, f32[512]{0:T(512)S(1)} %add_bitcast_fusion, f32[1024]{0:T(1024)S(1)} %bitcast.50, s32[512]{0:T(512)S(1)} %fusion.25), kind=kOutput, calls=%fused_computation.9 | convolution fusion | flops 1078460416 | bytes 4206592 | tf_op jit(solution)/shard_map/dot_general | solution.py:109
  115.0 1.3 fusion.41
  116.6 1.3 fusion
  121.0 2.4 %collective-permute-start.7 = (f32[512,1024]{1,0:T(8,128)S(1)}, f32[512,1024]{1,0:T(8,128)S(1)}, u32[]{:S(2)}, u32[]{:S(2)}) collective-permute-start(f32[512,1024]{1,0:T(8,128)S(1)} %add_add_fusion), channel_id=1, source_target_pairs={{0,8},{8,0},{1,9},{9,1},{2,10},{10,2},{3,11},{11,3},{4,12},{12,4},... | collective-permute-start | bytes 6291464 | tf_op jit(solution)/shard_map/ppermute | solution.py:24
  125.7 1.4 collective-permute-done.7
  128.4 18.2 %all_to_all.36 = bf16[16,256,128]{2,1,0:T(8,128)(2,1)S(1)} all-to-all(bf16[16,256,128]{2,1,0:T(8,128)(2,1)S(1)} %bitcast.42), channel_id=1, replica_groups=mesh['x_lo'=2,'z_hi'=4,'z_lo'=4,'core'=2,'y'=4,'x_hi'=2] {'x_lo','y','x_..., dimensions={0} | all-to-all | bytes 2097152 | tf_op jit(solution)/shard_map/all_to_all | solution.py:16
  146.7 14.6 %all_to_all.37 = f32[16,16,128]{2,1,0:T(8,128)S(1)} all-to-all(f32[16,16,128]{2,1,0:T(8,128)S(1)} %bitcast.45), channel_id=1, replica_groups=mesh['x_lo'=2,'z_hi'=4,'z_lo'=4,'core'=2,'y'=4,'x_hi'=2] {'z_hi','z_lo'}, dimensions={0} | all-to-all | bytes 262144 | tf_op jit(solution)/shard_map/all_to_all | solution.py:16
  161.4 15.7 %all_to_all.38 = f32[16,16,128]{2,1,0:T(8,128)S(1)} all-to-all(f32[16,16,128]{2,1,0:T(8,128)S(1)} %broadcast_in_dim.20), channel_id=1, replica_groups=mesh['x_lo'=2,'z_hi'=4,'z_lo'=4,'core'=2,'y'=4,'x_hi'=2] {'z_hi','z_lo'}, dimensions={0} | all-to-all | bytes 262144 | tf_op jit(solution)/shard_map/all_to_all | solution.py:16
  177.1 15.0 %all_to_all.39 = f32[4,256,128]{2,1,0:T(8,128)S(1)} all-to-all(f32[4,256,128]{2,1,0:T(8,128)S(1)} %broadcast_in_dim.22), channel_id=1, replica_groups=mesh['x_lo'=2,'z_hi'=4,'z_lo'=4,'core'=2,'y'=4,'x_hi'=2] {'core','x_lo'}, dimensions={0} | all-to-all | bytes 1048576 | tf_op jit(solution)/shard_map/all_to_all | solution.py:16
  (72 shorter events, 12.3 us)
Async XLA Ops:
  0.0 1.0 copy-start
  0.0 17.9 %copy-start.10 = (bf16[1024,128]{1,0:T(8,128)(2,1)S(1)}, bf16[1024,128]{1,0:T(8,128)(2,1)}, u32[]{:S(2)}) copy-start(bf16[1024,128]{1,0:T(8,128)(2,1)} %param.6) | copy-start | bytes 786436
  1.0 24.2 %copy-start.8 = (bf16[256,1024]{1,0:T(8,128)(2,1)S(1)}, bf16[256,1024]{1,0:T(8,128)(2,1)}, u32[]{:S(2)}) copy-start(bf16[256,1024]{1,0:T(8,128)(2,1)} %param.4) | copy-start | bytes 1572868
  2.2 60.6 %all-to-all-start = ((bf16[16,32,1024]{2,1,0:T(8,128)(2,1)}), bf16[16,32,1024]{2,1,0:T(8,128)(2,1)S(1)}, u32[]{:S(2)}, u32[]{:S(2)}) async-start(bf16[16,32,1024]{2,1,0:T(8,128)(2,1)} %broadcast_in_dim.15), calls=%async_computation | async-start | bytes 2097152 | tf_op jit(solution)/shard_map/all_to_all | solution.py:16
  17.9 7.2 %collective-permute-start = (bf16[512,128]{1,0:T(8,128)(2,1)S(1)}, bf16[512,128]{1,0:T(8,128)(2,1)S(1)}, u32[]{:S(2)}, u32[]{:S(2)}) collective-permute-start(bf16[512,128]{1,0:T(8,128)(2,1)S(1)} %constant_dynamic-slice_fusion), channel_id=1, source_target_pairs={{0,1},{1,0},{2,3},{3,2},{4,5},{5,4},{6,7},{7,6},{8,9},{9,8},{10,11... | collective-permute-start | bytes 393224 | tf_op jit(solution)/shard_map/ppermute | solution.py:24
  25.3 13.9 %collective-permute-start.5 = (bf16[256,1024]{1,0:T(8,128)(2,1)S(1)}, bf16[256,1024]{1,0:T(8,128)(2,1)S(1)}, u32[]{:S(2)}, u32[]{:S(2)}) collective-permute-start(bf16[256,1024]{1,0:T(8,128)(2,1)S(1)} %copy-done.8), channel_id=1, source_target_pairs={{0,256},{256,0},{1,257},{257,1},{2,258},{258,2},{3,259},{259,3},{4... | collective-permute-start | bytes 1572872 | tf_op jit(solution)/shard_map/ppermute | solution.py:24
  28.4 17.1 %collective-permute-start.3 = (bf16[512,256]{1,0:T(8,128)(2,1)S(1)}, bf16[512,256]{1,0:T(8,128)(2,1)S(1)}, u32[]{:S(2)}, u32[]{:S(2)}) collective-permute-start(bf16[512,256]{1,0:T(8,128)(2,1)S(1)} %pad_maximum_fusion.2), channel_id=1, source_target_pairs={{6,0},{0,2},{2,4},{4,6},{7,1},{1,3},{3,5},{5,7},{14,8},{8,10},{10,... | collective-permute-start | bytes 786440 | tf_op jit(solution)/shard_map/ppermute | solution.py:29
  31.6 13.9 %collective-permute-start.2 = (bf16[512,256]{1,0:T(8,128)(2,1)S(1)}, bf16[512,256]{1,0:T(8,128)(2,1)S(1)}, u32[]{:S(2)}, u32[]{:S(2)}) collective-permute-start(bf16[512,256]{1,0:T(8,128)(2,1)S(1)} %pad_maximum_fusion.2), channel_id=1, source_target_pairs={{4,0},{6,2},{0,4},{2,6},{5,1},{7,3},{1,5},{3,7},{12,8},{14,10},{8,... | collective-permute-start | bytes 786440 | tf_op jit(solution)/shard_map/ppermute | solution.py:29
  36.2 10.2 %collective-permute-start.1 = (bf16[512,256]{1,0:T(8,128)(2,1)S(1)}, bf16[512,256]{1,0:T(8,128)(2,1)S(1)}, u32[]{:S(2)}, u32[]{:S(2)}) collective-permute-start(bf16[512,256]{1,0:T(8,128)(2,1)S(1)} %pad_maximum_fusion.2), channel_id=1, source_target_pairs={{2,0},{4,2},{6,4},{0,6},{3,1},{5,3},{7,5},{1,7},{10,8},{12,10},{14... | collective-permute-start | bytes 786440 | tf_op jit(solution)/shard_map/ppermute | solution.py:29
  39.1 7.3 %copy-start.9 = (bf16[256,1024]{1,0:T(8,128)(2,1)}, bf16[256,1024]{1,0:T(8,128)(2,1)S(1)}, u32[]{:S(2)}) copy-start(bf16[256,1024]{1,0:T(8,128)(2,1)S(1)} %collective-permute-done.5) | copy-start | bytes 1572868
  40.3 11.6 %collective-permute-start.6 = (bf16[512,1024]{1,0:T(8,128)(2,1)}, bf16[512,1024]{1,0:T(8,128)(2,1)}, u32[]{:S(2)}, u32[]{:S(2)}) collective-permute-start(bf16[512,1024]{1,0:T(8,128)(2,1)} %pad_maximum_fusion.1), channel_id=1, source_target_pairs={{0,8},{8,0},{1,9},{9,1},{2,10},{10,2},{3,11},{11,3},{4,12},{12,4},... | collective-permute-start | bytes 3145736 | tf_op jit(solution)/shard_map/ppermute | solution.py:24
  46.5 6.7 %copy-start.1 = (bf16[4,512,256]{2,1,0:T(8,128)(2,1)}, bf16[4,512,256]{2,1,0:T(8,128)(2,1)S(1)}, u32[]{:S(2)}) copy-start(bf16[4,512,256]{2,1,0:T(8,128)(2,1)S(1)} %pad_maximum_fusion.near_ref) | copy-start | bytes 3145732
  46.5 6.7 %collective-permute-start.4 = (bf16[4,512,256]{2,1,0:T(8,128)(2,1)S(1)}, bf16[4,512,256]{2,1,0:T(8,128)(2,1)}, u32[]{:S(2)}, u32[]{:S(2)}) collective-permute-start(bf16[4,512,256]{2,1,0:T(8,128)(2,1)S(1)} %pad_maximum_fusion.near_ref), channel_id=1, source_target_pairs={{0,8},{8,0},{1,9},{9,1},{2,10},{10,2},{3,11},{11,3},{4,12},{12,4},... | collective-permute-start | bytes 3145736 | tf_op jit(solution)/shard_map/ppermute | solution.py:24
  57.5 1.4 copy-start.3
  58.9 1.3 copy-start.5
  62.8 1.2 copy-start.2
  64.0 2.9 %copy-start.6 = (bf16[1024,1024]{1,0:T(8,128)(2,1)S(1)}, bf16[1024,1024]{1,0:T(8,128)(2,1)}, u32[]{:S(2)}) copy-start(bf16[1024,1024]{1,0:T(8,128)(2,1)} %copy-done.5) | copy-start | bytes 6291460
  68.3 43.1 %copy-start.11 = (s32[256]{0:T(256)S(1)}, s32[256]{0:T(256)}, u32[]{:S(2)}) copy-start(s32[256]{0:T(256)} %param.7) | copy-start | bytes 3076
  94.4 16.6 %all-to-all-start.2 = ((f32[32,8,128]{2,1,0:T(8,128)}), f32[32,8,128]{2,1,0:T(8,128)S(1)}, u32[]{:S(2)}, u32[]{:S(2)}) async-start(f32[32,8,128]{2,1,0:T(8,128)} %broadcast_in_dim.17), calls=%async_computation.2 | async-start | bytes 262144 | tf_op jit(solution)/shard_map/all_to_all | solution.py:16
  111.3 3.6 %copy-start.7 = (bf16[1024,1024]{1,0:T(8,128)(2,1)S(1)}, bf16[1024,1024]{1,0:T(8,128)(2,1)}, u32[]{:S(2)}) copy-start(bf16[1024,1024]{1,0:T(8,128)(2,1)} %copy-done.5) | copy-start | bytes 6291460
  115.0 1.6 copy-start.4
  121.0 6.1 %collective-permute-start.7 = (f32[512,1024]{1,0:T(8,128)S(1)}, f32[512,1024]{1,0:T(8,128)S(1)}, u32[]{:S(2)}, u32[]{:S(2)}) collective-permute-start(f32[512,1024]{1,0:T(8,128)S(1)} %add_add_fusion), channel_id=1, source_target_pairs={{0,8},{8,0},{1,9},{9,1},{2,10},{10,2},{3,11},{11,3},{4,12},{12,4},... | collective-permute-start | bytes 6291464 | tf_op jit(solution)/shard_map/ppermute | solution.py:24

commit v4 on v3

--- a/solution.py
+++ b/solution.py
@@ -81,7 +81,7 @@
             bytes_accessed=2 * (rows * depth + depth * width + rows * width),
             transcendentals=0,
         ),
-        compiler_params=pltpu.CompilerParams(vmem_limit_bytes=12 * 2**20),
+        compiler_params=pltpu.CompilerParams(vmem_limit_bytes=8 * 2**20),
     )(at, x, near, far)
 
 
@@ -138,9 +138,14 @@
     col_part = log_sum_exp(scores, 1).reshape(-1, 128)
     row_part = own_first(log_sum_exp(scores, 0).reshape(2, 2, rows)).reshape(-1, 128)
     col_part, row_part = lax.optimization_barrier((col_part, row_part))
-    cols = from_all(col_part, LAYERS)
-    cols, row_part, positives = lax.optimization_barrier((cols, row_part, positives))
+    core = lax.axis_index("core")
+    half = depth // 2
+    given, own = ((1 - core) * half).astype(jnp.uint32), (core * half).astype(jnp.uint32)
+    layer, start = lax.axis_index(LAYERS), cut * chunk
+
     all_rows = from_all(row_part, PLANE)
+    places = (given + 2 * own).astype(jnp.float32) + (layer + start).astype(jnp.float32)
+    cols = from_all(col_part + 0.0 * places, LAYERS)
     cols, all_rows, positives, refusal_emb = lax.optimization_barrier(
         (cols, all_rows, positives, refusal_emb)
     )
@@ -148,8 +153,8 @@
     col_lse = log_sum_exp(cols, 0).reshape(n_keys)
 
     pair = jnp.concatenate([positives, jnp.full((n_queries - rows,), -1, jnp.int32)])
-    key = jnp.arange(n_keys, dtype=jnp.int32)
-    place = jnp.where(key // chunk == lax.axis_index(LAYERS), cut * chunk + key % chunk, -2)
+    key = jnp.arange(n_keys, dtype=jnp.int32) + (0.0 * col_lse).astype(jnp.int32)
+    place = jnp.where(key // chunk == layer, start + key % chunk, -2)
     marks = (pair[None, :] == place[:, None]).astype(jnp.float32)
     scores = score(refusal_emb, prompt_emb, inv_scale)
     probs = jnp.exp(scores - row_lse[None, :]) + jnp.exp(scores - col_lse[:, None])
@@ -170,10 +175,8 @@
             + (dot_first(left[1], refusal_emb) + dot_first(right, refusal_grad[1]))
         )
 
-    core = lax.axis_index("core")
-    half = depth // 2
-    came = from_twin(product((1 - core) * half, half), "core")
-    kept = (product(core * half, half) + came).astype(jnp.bfloat16)
+    came = from_twin(product(given, half), "core")
+    kept = (product(own, half) + came).astype(jnp.bfloat16)
     parts = lax.axis_size("x_lo")
     pieces = kept.reshape(parts, half // parts, cuts, width // cuts).transpose(0, 2, 1, 3)
     pieces = pieces.reshape(parts * cuts, half // parts, width // cuts)

time: 194 us -> 194 us (level)
  blocking collectives: 88 us -> 104 us
  starting transfers between devices: 54.9 us -> 45.9 us
  waiting for transfers between devices: 14.9 us -> 7.07 us
    all_to_all x5 -> x6, blocking collectives: 88 us -> 104 us  [exchange(): return lax.all_to_all(x, axes, split_axis=0, concat_axis=0, tiled=True)]
    all_to_all x2 -> x1, starting transfers between devices: 24.7 us -> 15.7 us  [exchange(): return lax.all_to_all(x, axes, split_axis=0, concat_axis=0, tiled=True)]
    all_to_all x2 -> x1, waiting for transfers between devices: 10.1 us -> 2.56 us  [exchange(): return lax.all_to_all(x, axes, split_axis=0, concat_axis=0, tiled=True)]
  transfers between devices with their start and end apart: 10 -> 9, of which waited for: 5 -> 4; matrix products, arithmetic and copies ran while one was open for 3% -> 3% of each run, Pallas kernels for 2% -> 2%
where the time goes in v4:
time: 194 us; the launch traced here: 193 us
  blocking collectives  104 us (54%)
  starting transfers between devices  45.9 us (24%)
  matrix products  14.9 us (8%)
  local copies, waits for them, and re-layouts  10.3 us (5%)
  Pallas kernels  7.15 us (4%)
  waiting for transfers between devices  7.07 us (4%)
  other arithmetic  2.71 us (1%)
    all_to_all x6, blocking collectives, exchange(): return lax.all_to_all(x, axes, split_axis=0, concat_axis=0, tiled=True)  104 us
    ppermute x5, starting transfers between devices, from_twin(): return lax.ppermute(x, axis, [(0, 1), (1, 0)])  19.4 us
    all_to_all x1, starting transfers between devices, exchange(): return lax.all_to_all(x, axes, split_axis=0, concat_axis=0, tiled=True)  15.7 us
    ppermute x3, starting transfers between devices, from_ahead(): lax.ppermute(x, axis, [((i + by) % devices, i) for i in range(devices)])  10.7 us
    unnamed x29, local copies, waits for them, and re-layouts  7.43 us
    dot_general x8, matrix products, dot_first(): lax.dot_general(a, b, (((0,), (0,)), ((), ())), preferred_element_type=jn...  7.36 us
    pallas_call x2, Pallas kernels, project(): pl.pallas_call(project_kernel, grid=(rows // block,), out_shape=jax.Shape...  7.15 us
    dot_general x2, matrix products, score(): lax.dot_general(refusal_emb, prompt_emb, (((1,), (1,)), ((), ())), prefer...  4.99 us
  transfers between devices with their start and end apart: 9, of which 4 were waited for; matrix products, arithmetic and copies ran while one was open for 3% of the time, Pallas kernels for 2%

profile of v4, /device:TPU:1, one launch (start us, length us, event | category | flops | bytes accessed | tf_op | source)
XLA Modules:
  0.0 192.8 jit_solution(4843352176268424735)
XLA Ops:
  1.1 1.1 broadcast_in_dim.15
  2.2 15.7 %all-to-all-start = ((bf16[16,32,1024]{2,1,0:T(8,128)(2,1)}), bf16[16,32,1024]{2,1,0:T(8,128)(2,1)S(1)}, u32[]{:S(2)}, u32[]{:S(2)}) async-start(bf16[16,32,1024]{2,1,0:T(8,128)(2,1)} %broadcast_in_dim.15), calls=%async_computation | async-start | bytes 2097152 | tf_op jit(solution)/shard_map/all_to_all | solution.py:16
  17.9 4.7 %collective-permute-start = (bf16[512,128]{1,0:T(8,128)(2,1)S(1)}, bf16[512,128]{1,0:T(8,128)(2,1)S(1)}, u32[]{:S(2)}, u32[]{:S(2)}) collective-permute-start(bf16[512,128]{1,0:T(8,128)(2,1)S(1)} %constant_dynamic-slice_fusion), channel_id=1, source_target_pairs={{0,1},{1,0},{2,3},{3,2},{4,5},{5,4},{6,7},{7,6},{8,9},{9,8},{10,11... | collective-permute-start | bytes 393224 | tf_op jit(solution)/shard_map/ppermute | solution.py:24
  22.6 2.6 %collective-permute-done = bf16[512,128]{1,0:T(8,128)(2,1)S(1)} collective-permute-done((bf16[512,128]{1,0:T(8,128)(2,1)S(1)}, bf16[512,128]{1,0:T(8,128)(2,1)S(1)}, u32[]{:S(2)}, u32[]{:S(2)}) %collective-permute-start) | collective-permute-done | bytes 131104 | tf_op jit(solution)/shard_map/ppermute | solution.py:24
  25.3 3.1 %collective-permute-start.5 = (bf16[256,1024]{1,0:T(8,128)(2,1)S(1)}, bf16[256,1024]{1,0:T(8,128)(2,1)S(1)}, u32[]{:S(2)}, u32[]{:S(2)}) collective-permute-start(bf16[256,1024]{1,0:T(8,128)(2,1)S(1)} %copy-done.8), channel_id=1, source_target_pairs={{0,256},{256,0},{1,257},{257,1},{2,258},{258,2},{3,259},{259,3},{4... | collective-permute-start | bytes 1572872 | tf_op jit(solution)/shard_map/ppermute | solution.py:24
  28.4 3.2 %collective-permute-start.3 = (bf16[512,256]{1,0:T(8,128)(2,1)S(1)}, bf16[512,256]{1,0:T(8,128)(2,1)S(1)}, u32[]{:S(2)}, u32[]{:S(2)}) collective-permute-start(bf16[512,256]{1,0:T(8,128)(2,1)S(1)} %pad_maximum_fusion.2), channel_id=1, source_target_pairs={{6,0},{0,2},{2,4},{4,6},{7,1},{1,3},{3,5},{5,7},{14,8},{8,10},{10,... | collective-permute-start | bytes 786440 | tf_op jit(solution)/shard_map/ppermute | solution.py:29
  31.6 4.5 %collective-permute-start.2 = (bf16[512,256]{1,0:T(8,128)(2,1)S(1)}, bf16[512,256]{1,0:T(8,128)(2,1)S(1)}, u32[]{:S(2)}, u32[]{:S(2)}) collective-permute-start(bf16[512,256]{1,0:T(8,128)(2,1)S(1)} %pad_maximum_fusion.2), channel_id=1, source_target_pairs={{4,0},{6,2},{0,4},{2,6},{5,1},{7,3},{1,5},{3,7},{12,8},{14,10},{8,... | collective-permute-start | bytes 786440 | tf_op jit(solution)/shard_map/ppermute | solution.py:29
  36.1 3.0 %collective-permute-start.1 = (bf16[512,256]{1,0:T(8,128)(2,1)S(1)}, bf16[512,256]{1,0:T(8,128)(2,1)S(1)}, u32[]{:S(2)}, u32[]{:S(2)}) collective-permute-start(bf16[512,256]{1,0:T(8,128)(2,1)S(1)} %pad_maximum_fusion.2), channel_id=1, source_target_pairs={{2,0},{4,2},{6,4},{0,6},{3,1},{5,3},{7,5},{1,7},{10,8},{12,10},{14... | collective-permute-start | bytes 786440 | tf_op jit(solution)/shard_map/ppermute | solution.py:29
  39.2 1.2 pad_maximum_fusion.1
  40.3 5.1 %collective-permute-start.6 = (bf16[512,1024]{1,0:T(8,128)(2,1)}, bf16[512,1024]{1,0:T(8,128)(2,1)}, u32[]{:S(2)}, u32[]{:S(2)}) collective-permute-start(bf16[512,1024]{1,0:T(8,128)(2,1)} %pad_maximum_fusion.1), channel_id=1, source_target_pairs={{0,8},{8,0},{1,9},{9,1},{2,10},{10,2},{3,11},{11,3},{4,12},{12,4},... | collective-permute-start | bytes 3145736 | tf_op jit(solution)/shard_map/ppermute | solution.py:24
  46.5 4.2 %collective-permute-start.4 = (bf16[4,512,256]{2,1,0:T(8,128)(2,1)S(1)}, bf16[4,512,256]{2,1,0:T(8,128)(2,1)}, u32[]{:S(2)}, u32[]{:S(2)}) collective-permute-start(bf16[4,512,256]{2,1,0:T(8,128)(2,1)S(1)} %pad_maximum_fusion.near_ref), channel_id=1, source_target_pairs={{0,8},{8,0},{1,9},{9,1},{2,10},{10,2},{3,11},{11,3},{4,12},{12,4},... | collective-permute-start | bytes 3145736 | tf_op jit(solution)/shard_map/ppermute | solution.py:24
  50.9 1.1 constant_dynamic-update-slice_fusion.1
  52.0 1.3 constant_dynamic-update-slice_fusion.x_ref
  53.3 4.3 %shard_map.47 = bf16[1024,1024]{1,0:T(8,128)(2,1)S(1)} custom-call(s32[2]{0:T(128)S(1)} %pad_add_fusion.at_ref, bf16[1024,1024]{1,0:T(8,128)(2,1)S(1)} %constant_dynamic-update-slice_fusion.x_ref, bf16[4,512,256]{2,1,0:T(8,128)(2,1)S(1)} %pad_maximum_fusion.near_ref, bf16[4,512,256]{2,1,0:T(8,128)(2,1)} %collective-permute-done.4.far_ref), custom_call_target="tpu_custom_call" | custom-call | flops 2147483648 | bytes 6291456 | tf_op jit(solution)/shard_map/pallas_call | solution.py:68
  57.6 1.3 copy-done.3
  58.9 1.3 copy-done.5
  60.2 2.6 %all-to-all-done = bf16[16,32,1024]{2,1,0:T(8,128)(2,1)S(1)} async-done(((bf16[16,32,1024]{2,1,0:T(8,128)(2,1)}), bf16[16,32,1024]{2,1,0:T(8,128)(2,1)S(1)}, u32[]{:S(2)}, u32[]{:S(2)}) %all-to-all-start) | async-done | bytes 1048608 | tf_op jit(solution)/shard_map/all_to_all | solution.py:16
  62.8 1.2 copy-done.2
  64.0 2.9 %shard_map.46 = bf16[512,1024]{1,0:T(8,128)(2,1)S(1)} custom-call(s32[2]{0:T(128)S(1)} %pad_add_fusion.at_ref, bf16[512,1024]{1,0:T(8,128)(2,1)S(1)} %bitcast.37, bf16[4,512,256]{2,1,0:T(8,128)(2,1)S(1)} %copy-done.2, bf16[4,512,256]{2,1,0:T(8,128)(2,1)} %collective-permute-done.4.far_ref), custom_call_target="tpu_custom_call" | custom-call | flops 1073741824 | bytes 4194304 | tf_op jit(solution)/shard_map/pallas_call | solution.py:68
  66.9 1.4 multiply_reduce_fusion
  69.3 24.5 %all_to_all.35 = f32[16,4,128]{2,1,0:T(4,128)S(1)} all-to-all(f32[16,4,128]{2,1,0:T(4,128)S(1)} %broadcast_in_dim.16), channel_id=1, replica_groups=mesh['x_lo'=2,'z_hi'=4,'z_lo'=4,'core'=2,'y'=4,'x_hi'=2] {'z_hi','z_lo'}, dimensions={0} | all-to-all | bytes 65536 | tf_op jit(solution)/shard_map/all_to_all | solution.py:16
  93.8 16.3 %all_to_all.36 = f32[32,8,128]{2,1,0:T(8,128)S(1)} all-to-all(f32[32,8,128]{2,1,0:T(8,128)S(1)} %broadcast_in_dim.17), channel_id=1, replica_groups=mesh['x_lo'=2,'z_hi'=4,'z_lo'=4,'core'=2,'y'=4,'x_hi'=2] {'core','x_lo',..., dimensions={0} | all-to-all | bytes 262144 | tf_op jit(solution)/shard_map/all_to_all | solution.py:16
  110.5 3.6 %multiply_convert_fusion = bf16[512,1024]{1,0:T(8,128)(2,1)S(1)} fusion(bf16[512,1024]{1,0:T(8,128)(2,1)S(1)} %shard_map.46, bf16[1024,1024]{1,0:T(8,128)(2,1)} %copy-done.5, s32[1024]{0:T(1024)S(1)} %concatenate.16, f32[512]{0:T(512)S(1)} %get-tuple-element.26, f32[1024]{0:T(1024)S(1)} %bitcast.51, s32[512]{0:T(512)S(1)} %get-tuple-element.25), kind=kOutput, calls=%fused_computation.9 | convolution fusion | flops 1078460416 | bytes 4206592 | tf_op jit(solution)/shard_map/dot_general | solution.py:109
  114.1 1.3 fusion.36
  115.7 1.3 fusion
  120.6 2.3 %collective-permute-start.7 = (f32[512,1024]{1,0:T(8,128)S(1)}, f32[512,1024]{1,0:T(8,128)S(1)}, u32[]{:S(2)}, u32[]{:S(2)}) collective-permute-start(f32[512,1024]{1,0:T(8,128)S(1)} %add_add_fusion), channel_id=1, source_target_pairs={{0,8},{8,0},{1,9},{9,1},{2,10},{10,2},{3,11},{11,3},{4,12},{12,4},... | collective-permute-start | bytes 6291464 | tf_op jit(solution)/shard_map/ppermute | solution.py:24
  125.6 1.1 collective-permute-done.7
  126.7 1.1 fusion.2
  128.3 18.2 %all_to_all.37 = bf16[16,256,128]{2,1,0:T(8,128)(2,1)S(1)} all-to-all(bf16[16,256,128]{2,1,0:T(8,128)(2,1)S(1)} %bitcast.43), channel_id=1, replica_groups=mesh['x_lo'=2,'z_hi'=4,'z_lo'=4,'core'=2,'y'=4,'x_hi'=2] {'x_lo','y','x_..., dimensions={0} | all-to-all | bytes 2097152 | tf_op jit(solution)/shard_map/all_to_all | solution.py:16
  146.6 14.6 %all_to_all.38 = f32[16,16,128]{2,1,0:T(8,128)S(1)} all-to-all(f32[16,16,128]{2,1,0:T(8,128)S(1)} %bitcast.46), channel_id=1, replica_groups=mesh['x_lo'=2,'z_hi'=4,'z_lo'=4,'core'=2,'y'=4,'x_hi'=2] {'z_hi','z_lo'}, dimensions={0} | all-to-all | bytes 262144 | tf_op jit(solution)/shard_map/all_to_all | solution.py:16
  161.2 15.7 %all_to_all.39 = f32[16,16,128]{2,1,0:T(8,128)S(1)} all-to-all(f32[16,16,128]{2,1,0:T(8,128)S(1)} %broadcast_in_dim.20), channel_id=1, replica_groups=mesh['x_lo'=2,'z_hi'=4,'z_lo'=4,'core'=2,'y'=4,'x_hi'=2] {'z_hi','z_lo'}, dimensions={0} | all-to-all | bytes 262144 | tf_op jit(solution)/shard_map/all_to_all | solution.py:16
  177.0 15.0 %all_to_all.40 = f32[4,256,128]{2,1,0:T(8,128)S(1)} all-to-all(f32[4,256,128]{2,1,0:T(8,128)S(1)} %broadcast_in_dim.22), channel_id=1, replica_groups=mesh['x_lo'=2,'z_hi'=4,'z_lo'=4,'core'=2,'y'=4,'x_hi'=2] {'core','x_lo'}, dimensions={0} | all-to-all | bytes 1048576 | tf_op jit(solution)/shard_map/all_to_all | solution.py:16
  (71 shorter events, 11.7 us)
Async XLA Ops:
  0.0 1.0 copy-start
  0.0 17.9 %copy-start.10 = (bf16[1024,128]{1,0:T(8,128)(2,1)S(1)}, bf16[1024,128]{1,0:T(8,128)(2,1)}, u32[]{:S(2)}) copy-start(bf16[1024,128]{1,0:T(8,128)(2,1)} %param.6) | copy-start | bytes 786436
  1.0 24.2 %copy-start.8 = (bf16[256,1024]{1,0:T(8,128)(2,1)S(1)}, bf16[256,1024]{1,0:T(8,128)(2,1)}, u32[]{:S(2)}) copy-start(bf16[256,1024]{1,0:T(8,128)(2,1)} %param.4) | copy-start | bytes 1572868
  2.2 60.6 %all-to-all-start = ((bf16[16,32,1024]{2,1,0:T(8,128)(2,1)}), bf16[16,32,1024]{2,1,0:T(8,128)(2,1)S(1)}, u32[]{:S(2)}, u32[]{:S(2)}) async-start(bf16[16,32,1024]{2,1,0:T(8,128)(2,1)} %broadcast_in_dim.15), calls=%async_computation | async-start | bytes 2097152 | tf_op jit(solution)/shard_map/all_to_all | solution.py:16
  17.9 7.2 %collective-permute-start = (bf16[512,128]{1,0:T(8,128)(2,1)S(1)}, bf16[512,128]{1,0:T(8,128)(2,1)S(1)}, u32[]{:S(2)}, u32[]{:S(2)}) collective-permute-start(bf16[512,128]{1,0:T(8,128)(2,1)S(1)} %constant_dynamic-slice_fusion), channel_id=1, source_target_pairs={{0,1},{1,0},{2,3},{3,2},{4,5},{5,4},{6,7},{7,6},{8,9},{9,8},{10,11... | collective-permute-start | bytes 393224 | tf_op jit(solution)/shard_map/ppermute | solution.py:24
  25.3 13.9 %collective-permute-start.5 = (bf16[256,1024]{1,0:T(8,128)(2,1)S(1)}, bf16[256,1024]{1,0:T(8,128)(2,1)S(1)}, u32[]{:S(2)}, u32[]{:S(2)}) collective-permute-start(bf16[256,1024]{1,0:T(8,128)(2,1)S(1)} %copy-done.8), channel_id=1, source_target_pairs={{0,256},{256,0},{1,257},{257,1},{2,258},{258,2},{3,259},{259,3},{4... | collective-permute-start | bytes 1572872 | tf_op jit(solution)/shard_map/ppermute | solution.py:24
  28.4 17.1 %collective-permute-start.3 = (bf16[512,256]{1,0:T(8,128)(2,1)S(1)}, bf16[512,256]{1,0:T(8,128)(2,1)S(1)}, u32[]{:S(2)}, u32[]{:S(2)}) collective-permute-start(bf16[512,256]{1,0:T(8,128)(2,1)S(1)} %pad_maximum_fusion.2), channel_id=1, source_target_pairs={{6,0},{0,2},{2,4},{4,6},{7,1},{1,3},{3,5},{5,7},{14,8},{8,10},{10,... | collective-permute-start | bytes 786440 | tf_op jit(solution)/shard_map/ppermute | solution.py:29
  31.6 13.9 %collective-permute-start.2 = (bf16[512,256]{1,0:T(8,128)(2,1)S(1)}, bf16[512,256]{1,0:T(8,128)(2,1)S(1)}, u32[]{:S(2)}, u32[]{:S(2)}) collective-permute-start(bf16[512,256]{1,0:T(8,128)(2,1)S(1)} %pad_maximum_fusion.2), channel_id=1, source_target_pairs={{4,0},{6,2},{0,4},{2,6},{5,1},{7,3},{1,5},{3,7},{12,8},{14,10},{8,... | collective-permute-start | bytes 786440 | tf_op jit(solution)/shard_map/ppermute | solution.py:29
  36.1 10.2 %collective-permute-start.1 = (bf16[512,256]{1,0:T(8,128)(2,1)S(1)}, bf16[512,256]{1,0:T(8,128)(2,1)S(1)}, u32[]{:S(2)}, u32[]{:S(2)}) collective-permute-start(bf16[512,256]{1,0:T(8,128)(2,1)S(1)} %pad_maximum_fusion.2), channel_id=1, source_target_pairs={{2,0},{4,2},{6,4},{0,6},{3,1},{5,3},{7,5},{1,7},{10,8},{12,10},{14... | collective-permute-start | bytes 786440 | tf_op jit(solution)/shard_map/ppermute | solution.py:29
  39.1 7.3 %copy-start.9 = (bf16[256,1024]{1,0:T(8,128)(2,1)}, bf16[256,1024]{1,0:T(8,128)(2,1)S(1)}, u32[]{:S(2)}) copy-start(bf16[256,1024]{1,0:T(8,128)(2,1)S(1)} %collective-permute-done.5) | copy-start | bytes 1572868
  40.3 11.6 %collective-permute-start.6 = (bf16[512,1024]{1,0:T(8,128)(2,1)}, bf16[512,1024]{1,0:T(8,128)(2,1)}, u32[]{:S(2)}, u32[]{:S(2)}) collective-permute-start(bf16[512,1024]{1,0:T(8,128)(2,1)} %pad_maximum_fusion.1), channel_id=1, source_target_pairs={{0,8},{8,0},{1,9},{9,1},{2,10},{10,2},{3,11},{11,3},{4,12},{12,4},... | collective-permute-start | bytes 3145736 | tf_op jit(solution)/shard_map/ppermute | solution.py:24
  46.5 6.8 %copy-start.1 = (bf16[4,512,256]{2,1,0:T(8,128)(2,1)}, bf16[4,512,256]{2,1,0:T(8,128)(2,1)S(1)}, u32[]{:S(2)}) copy-start(bf16[4,512,256]{2,1,0:T(8,128)(2,1)S(1)} %pad_maximum_fusion.near_ref) | copy-start | bytes 3145732
  46.5 6.8 %collective-permute-start.4 = (bf16[4,512,256]{2,1,0:T(8,128)(2,1)S(1)}, bf16[4,512,256]{2,1,0:T(8,128)(2,1)}, u32[]{:S(2)}, u32[]{:S(2)}) collective-permute-start(bf16[4,512,256]{2,1,0:T(8,128)(2,1)S(1)} %pad_maximum_fusion.near_ref), channel_id=1, source_target_pairs={{0,8},{8,0},{1,9},{9,1},{2,10},{10,2},{3,11},{11,3},{4,12},{12,4},... | collective-permute-start | bytes 3145736 | tf_op jit(solution)/shard_map/ppermute | solution.py:24
  57.6 1.4 copy-start.3
  58.9 1.3 copy-start.5
  62.8 1.2 copy-start.2
  64.0 2.9 %copy-start.6 = (bf16[1024,1024]{1,0:T(8,128)(2,1)S(1)}, bf16[1024,1024]{1,0:T(8,128)(2,1)}, u32[]{:S(2)}) copy-start(bf16[1024,1024]{1,0:T(8,128)(2,1)} %copy-done.5) | copy-start | bytes 6291460
  68.3 42.2 %copy-start.11 = (s32[256]{0:T(256)S(1)}, s32[256]{0:T(256)}, u32[]{:S(2)}) copy-start(s32[256]{0:T(256)} %param.7) | copy-start | bytes 3076
  110.5 3.6 %copy-start.7 = (bf16[1024,1024]{1,0:T(8,128)(2,1)S(1)}, bf16[1024,1024]{1,0:T(8,128)(2,1)}, u32[]{:S(2)}) copy-start(bf16[1024,1024]{1,0:T(8,128)(2,1)} %copy-done.5) | copy-start | bytes 6291460
  114.1 1.6 copy-start.4
  120.6 6.1 %collective-permute-start.7 = (f32[512,1024]{1,0:T(8,128)S(1)}, f32[512,1024]{1,0:T(8,128)S(1)}, u32[]{:S(2)}, u32[]{:S(2)}) collective-permute-start(f32[512,1024]{1,0:T(8,128)S(1)} %add_add_fusion), channel_id=1, source_target_pairs={{0,8},{8,0},{1,9},{9,1},{2,10},{10,2},{3,11},{11,3},{4,12},{12,4},... | collective-permute-start | bytes 6291464 | tf_op jit(solution)/shard_map/ppermute | solution.py:24

commit v5 on v4

--- a/solution.py
+++ b/solution.py
@@ -131,6 +131,8 @@
     prompts = jnp.concatenate([pair_of_shards, from_twin(pair_of_shards, "core")], 0)
 
     prompt_emb = project(prompts, near, far)
+    near = pltpu.with_memory_space_constraint(near, pltpu.HBM)
+    far = pltpu.with_memory_space_constraint(far, pltpu.HBM)
     refusal_emb = project(refusals, near, far)
     scores = score(refusal_emb, prompt_emb, inv_scale)
     n_keys, n_queries = scores.shape

time: 194 us -> 193 us (level)
    unnamed x29 -> x27, local copies, waits for them, and re-layouts: 7.43 us -> 6.2 us
where the time goes in v5:
time: 193 us; the launch traced here: 192 us
  blocking collectives  104 us (54%)
  starting transfers between devices  45.8 us (24%)
  matrix products  14.9 us (8%)
  local copies, waits for them, and re-layouts  9.09 us (5%)
  Pallas kernels  7.46 us (4%)
  waiting for transfers between devices  7.12 us (4%)
  other arithmetic  2.71 us (1%)
    all_to_all x6, blocking collectives, exchange(): return lax.all_to_all(x, axes, split_axis=0, concat_axis=0, tiled=True)  104 us
    ppermute x5, starting transfers between devices, from_twin(): return lax.ppermute(x, axis, [(0, 1), (1, 0)])  19.3 us
    all_to_all x1, starting transfers between devices, exchange(): return lax.all_to_all(x, axes, split_axis=0, concat_axis=0, tiled=True)  15.7 us
    ppermute x3, starting transfers between devices, from_ahead(): lax.ppermute(x, axis, [((i + by) % devices, i) for i in range(devices)])  10.7 us
    pallas_call x2, Pallas kernels, project(): pl.pallas_call(project_kernel, grid=(rows // block,), out_shape=jax.Shape...  7.46 us
    dot_general x8, matrix products, dot_first(): lax.dot_general(a, b, (((0,), (0,)), ((), ())), preferred_element_type=jn...  7.35 us
    unnamed x27, local copies, waits for them, and re-layouts  6.2 us
    dot_general x2, matrix products, score(): lax.dot_general(refusal_emb, prompt_emb, (((1,), (1,)), ((), ())), prefer...  4.98 us
  transfers between devices with their start and end apart: 9, of which 4 were waited for; matrix products, arithmetic and copies ran while one was open for 3% of the time, Pallas kernels for 2%

profile of v5, /device:TPU:1, one launch (start us, length us, event | category | flops | bytes accessed | tf_op | source)
XLA Modules:
  0.0 191.9 jit_solution(2194136365149105139)
XLA Ops:
  0.0 1.0 copy-done
  1.1 1.1 broadcast_in_dim.15
  2.2 15.7 %all-to-all-start = ((bf16[16,32,1024]{2,1,0:T(8,128)(2,1)}), bf16[16,32,1024]{2,1,0:T(8,128)(2,1)S(1)}, u32[]{:S(2)}, u32[]{:S(2)}) async-start(bf16[16,32,1024]{2,1,0:T(8,128)(2,1)} %broadcast_in_dim.15), calls=%async_computation | async-start | bytes 2097152 | tf_op jit(solution)/shard_map/all_to_all | solution.py:16
  17.9 4.7 %collective-permute-start = (bf16[512,128]{1,0:T(8,128)(2,1)S(1)}, bf16[512,128]{1,0:T(8,128)(2,1)S(1)}, u32[]{:S(2)}, u32[]{:S(2)}) collective-permute-start(bf16[512,128]{1,0:T(8,128)(2,1)S(1)} %constant_dynamic-slice_fusion), channel_id=1, source_target_pairs={{0,1},{1,0},{2,3},{3,2},{4,5},{5,4},{6,7},{7,6},{8,9},{9,8},{10,11... | collective-permute-start | bytes 393224 | tf_op jit(solution)/shard_map/ppermute | solution.py:24
  22.6 2.6 %collective-permute-done = bf16[512,128]{1,0:T(8,128)(2,1)S(1)} collective-permute-done((bf16[512,128]{1,0:T(8,128)(2,1)S(1)}, bf16[512,128]{1,0:T(8,128)(2,1)S(1)}, u32[]{:S(2)}, u32[]{:S(2)}) %collective-permute-start) | collective-permute-done | bytes 131104 | tf_op jit(solution)/shard_map/ppermute | solution.py:24
  25.3 3.1 %collective-permute-start.5 = (bf16[256,1024]{1,0:T(8,128)(2,1)S(1)}, bf16[256,1024]{1,0:T(8,128)(2,1)S(1)}, u32[]{:S(2)}, u32[]{:S(2)}) collective-permute-start(bf16[256,1024]{1,0:T(8,128)(2,1)S(1)} %copy-done.7), channel_id=1, source_target_pairs={{0,256},{256,0},{1,257},{257,1},{2,258},{258,2},{3,259},{259,3},{4... | collective-permute-start | bytes 1572872 | tf_op jit(solution)/shard_map/ppermute | solution.py:24
  28.4 3.2 %collective-permute-start.3 = (bf16[512,256]{1,0:T(8,128)(2,1)S(1)}, bf16[512,256]{1,0:T(8,128)(2,1)S(1)}, u32[]{:S(2)}, u32[]{:S(2)}) collective-permute-start(bf16[512,256]{1,0:T(8,128)(2,1)S(1)} %pad_maximum_fusion.2), channel_id=1, source_target_pairs={{6,0},{0,2},{2,4},{4,6},{7,1},{1,3},{3,5},{5,7},{14,8},{8,10},{10,... | collective-permute-start | bytes 786440 | tf_op jit(solution)/shard_map/ppermute | solution.py:29
  31.6 4.5 %collective-permute-start.2 = (bf16[512,256]{1,0:T(8,128)(2,1)S(1)}, bf16[512,256]{1,0:T(8,128)(2,1)S(1)}, u32[]{:S(2)}, u32[]{:S(2)}) collective-permute-start(bf16[512,256]{1,0:T(8,128)(2,1)S(1)} %pad_maximum_fusion.2), channel_id=1, source_target_pairs={{4,0},{6,2},{0,4},{2,6},{5,1},{7,3},{1,5},{3,7},{12,8},{14,10},{8,... | collective-permute-start | bytes 786440 | tf_op jit(solution)/shard_map/ppermute | solution.py:29
  36.1 3.0 %collective-permute-start.1 = (bf16[512,256]{1,0:T(8,128)(2,1)S(1)}, bf16[512,256]{1,0:T(8,128)(2,1)S(1)}, u32[]{:S(2)}, u32[]{:S(2)}) collective-permute-start(bf16[512,256]{1,0:T(8,128)(2,1)S(1)} %pad_maximum_fusion.2), channel_id=1, source_target_pairs={{2,0},{4,2},{6,4},{0,6},{3,1},{5,3},{7,5},{1,7},{10,8},{12,10},{14... | collective-permute-start | bytes 786440 | tf_op jit(solution)/shard_map/ppermute | solution.py:29
  39.2 1.2 pad_maximum_fusion.1
  40.3 5.1 %collective-permute-start.6 = (bf16[512,1024]{1,0:T(8,128)(2,1)}, bf16[512,1024]{1,0:T(8,128)(2,1)}, u32[]{:S(2)}, u32[]{:S(2)}) collective-permute-start(bf16[512,1024]{1,0:T(8,128)(2,1)} %pad_maximum_fusion.1), channel_id=1, source_target_pairs={{0,8},{8,0},{1,9},{9,1},{2,10},{10,2},{3,11},{11,3},{4,12},{12,4},... | collective-permute-start | bytes 3145736 | tf_op jit(solution)/shard_map/ppermute | solution.py:24
  46.5 4.2 %collective-permute-start.4 = (bf16[4,512,256]{2,1,0:T(8,128)(2,1)S(1)}, bf16[4,512,256]{2,1,0:T(8,128)(2,1)}, u32[]{:S(2)}, u32[]{:S(2)}) collective-permute-start(bf16[4,512,256]{2,1,0:T(8,128)(2,1)S(1)} %pad_maximum_fusion.near_ref), channel_id=1, source_target_pairs={{0,8},{8,0},{1,9},{9,1},{2,10},{10,2},{3,11},{11,3},{4,12},{12,4},... | collective-permute-start | bytes 3145736 | tf_op jit(solution)/shard_map/ppermute | solution.py:24
  50.9 1.1 constant_dynamic-update-slice_fusion.1
  52.0 1.3 constant_dynamic-update-slice_fusion.x_ref
  53.3 4.3 %shard_map.47 = bf16[1024,1024]{1,0:T(8,128)(2,1)S(1)} custom-call(s32[2]{0:T(128)S(1)} %pad_add_fusion.at_ref, bf16[1024,1024]{1,0:T(8,128)(2,1)S(1)} %constant_dynamic-update-slice_fusion.x_ref, bf16[4,512,256]{2,1,0:T(8,128)(2,1)S(1)} %pad_maximum_fusion.near_ref, bf16[4,512,256]{2,1,0:T(8,128)(2,1)} %collective-permute-done.4.far_ref), custom_call_target="tpu_custom_call" | custom-call | flops 2147483648 | bytes 6291456 | tf_op jit(solution)/shard_map/pallas_call | solution.py:68
  57.6 1.3 copy-done.2
  58.9 1.3 copy-done.4
  60.2 2.6 %all-to-all-done = bf16[16,32,1024]{2,1,0:T(8,128)(2,1)S(1)} async-done(((bf16[16,32,1024]{2,1,0:T(8,128)(2,1)}), bf16[16,32,1024]{2,1,0:T(8,128)(2,1)S(1)}, u32[]{:S(2)}, u32[]{:S(2)}) %all-to-all-start) | async-done | bytes 1048608 | tf_op jit(solution)/shard_map/all_to_all | solution.py:16
  62.8 3.2 %shard_map.46 = bf16[512,1024]{1,0:T(8,128)(2,1)S(1)} custom-call(s32[2]{0:T(128)S(1)} %pad_add_fusion.at_ref, bf16[512,1024]{1,0:T(8,128)(2,1)S(1)} %bitcast.37, bf16[4,512,256]{2,1,0:T(8,128)(2,1)} %copy-done.1, bf16[4,512,256]{2,1,0:T(8,128)(2,1)} %collective-permute-done.4.far_ref), custom_call_target="tpu_custom_call" | custom-call | flops 1073741824 | bytes 4194304 | tf_op jit(solution)/shard_map/pallas_call | solution.py:68
  66.0 1.4 multiply_reduce_fusion
  68.4 24.5 %all_to_all.35 = f32[16,4,128]{2,1,0:T(4,128)S(1)} all-to-all(f32[16,4,128]{2,1,0:T(4,128)S(1)} %broadcast_in_dim.16), channel_id=1, replica_groups=mesh['x_lo'=2,'z_hi'=4,'z_lo'=4,'core'=2,'y'=4,'x_hi'=2] {'z_hi','z_lo'}, dimensions={0} | all-to-all | bytes 65536 | tf_op jit(solution)/shard_map/all_to_all | solution.py:16
  92.9 16.3 %all_to_all.36 = f32[32,8,128]{2,1,0:T(8,128)S(1)} all-to-all(f32[32,8,128]{2,1,0:T(8,128)S(1)} %broadcast_in_dim.17), channel_id=1, replica_groups=mesh['x_lo'=2,'z_hi'=4,'z_lo'=4,'core'=2,'y'=4,'x_hi'=2] {'core','x_lo',..., dimensions={0} | all-to-all | bytes 262144 | tf_op jit(solution)/shard_map/all_to_all | solution.py:16
  109.6 3.6 %multiply_convert_fusion = bf16[512,1024]{1,0:T(8,128)(2,1)S(1)} fusion(bf16[512,1024]{1,0:T(8,128)(2,1)S(1)} %shard_map.46, bf16[1024,1024]{1,0:T(8,128)(2,1)} %copy-done.4, s32[1024]{0:T(1024)S(1)} %concatenate.16, f32[512]{0:T(512)S(1)} %get-tuple-element.26, f32[1024]{0:T(1024)S(1)} %bitcast.51, s32[512]{0:T(512)S(1)} %get-tuple-element.25), kind=kOutput, calls=%fused_computation.9 | convolution fusion | flops 1078460416 | bytes 4206592 | tf_op jit(solution)/shard_map/dot_general | solution.py:109
  113.2 1.3 fusion.36
  114.8 1.3 fusion
  119.7 2.2 %collective-permute-start.7 = (f32[512,1024]{1,0:T(8,128)S(1)}, f32[512,1024]{1,0:T(8,128)S(1)}, u32[]{:S(2)}, u32[]{:S(2)}) collective-permute-start(f32[512,1024]{1,0:T(8,128)S(1)} %add_add_fusion), channel_id=1, source_target_pairs={{0,8},{8,0},{1,9},{9,1},{2,10},{10,2},{3,11},{11,3},{4,12},{12,4},... | collective-permute-start | bytes 6291464 | tf_op jit(solution)/shard_map/ppermute | solution.py:24
  124.7 1.1 collective-permute-done.7
  125.8 1.1 fusion.2
  127.3 18.2 %all_to_all.37 = bf16[16,256,128]{2,1,0:T(8,128)(2,1)S(1)} all-to-all(bf16[16,256,128]{2,1,0:T(8,128)(2,1)S(1)} %bitcast.43), channel_id=1, replica_groups=mesh['x_lo'=2,'z_hi'=4,'z_lo'=4,'core'=2,'y'=4,'x_hi'=2] {'x_lo','y','x_..., dimensions={0} | all-to-all | bytes 2097152 | tf_op jit(solution)/shard_map/all_to_all | solution.py:16
  145.7 14.6 %all_to_all.38 = f32[16,16,128]{2,1,0:T(8,128)S(1)} all-to-all(f32[16,16,128]{2,1,0:T(8,128)S(1)} %bitcast.46), channel_id=1, replica_groups=mesh['x_lo'=2,'z_hi'=4,'z_lo'=4,'core'=2,'y'=4,'x_hi'=2] {'z_hi','z_lo'}, dimensions={0} | all-to-all | bytes 262144 | tf_op jit(solution)/shard_map/all_to_all | solution.py:16
  160.3 15.7 %all_to_all.39 = f32[16,16,128]{2,1,0:T(8,128)S(1)} all-to-all(f32[16,16,128]{2,1,0:T(8,128)S(1)} %broadcast_in_dim.20), channel_id=1, replica_groups=mesh['x_lo'=2,'z_hi'=4,'z_lo'=4,'core'=2,'y'=4,'x_hi'=2] {'z_hi','z_lo'}, dimensions={0} | all-to-all | bytes 262144 | tf_op jit(solution)/shard_map/all_to_all | solution.py:16
  176.1 15.0 %all_to_all.40 = f32[4,256,128]{2,1,0:T(8,128)S(1)} all-to-all(f32[4,256,128]{2,1,0:T(8,128)S(1)} %broadcast_in_dim.22), channel_id=1, replica_groups=mesh['x_lo'=2,'z_hi'=4,'z_lo'=4,'core'=2,'y'=4,'x_hi'=2] {'core','x_lo'}, dimensions={0} | all-to-all | bytes 1048576 | tf_op jit(solution)/shard_map/all_to_all | solution.py:16
  (69 shorter events, 10.7 us)
Async XLA Ops:
  0.0 1.0 copy-start
  0.0 17.9 %copy-start.9 = (bf16[1024,128]{1,0:T(8,128)(2,1)S(1)}, bf16[1024,128]{1,0:T(8,128)(2,1)}, u32[]{:S(2)}) copy-start(bf16[1024,128]{1,0:T(8,128)(2,1)} %param.6) | copy-start | bytes 786436
  1.0 24.2 %copy-start.7 = (bf16[256,1024]{1,0:T(8,128)(2,1)S(1)}, bf16[256,1024]{1,0:T(8,128)(2,1)}, u32[]{:S(2)}) copy-start(bf16[256,1024]{1,0:T(8,128)(2,1)} %param.4) | copy-start | bytes 1572868
  2.2 60.6 %all-to-all-start = ((bf16[16,32,1024]{2,1,0:T(8,128)(2,1)}), bf16[16,32,1024]{2,1,0:T(8,128)(2,1)S(1)}, u32[]{:S(2)}, u32[]{:S(2)}) async-start(bf16[16,32,1024]{2,1,0:T(8,128)(2,1)} %broadcast_in_dim.15), calls=%async_computation | async-start | bytes 2097152 | tf_op jit(solution)/shard_map/all_to_all | solution.py:16
  17.9 7.2 %collective-permute-start = (bf16[512,128]{1,0:T(8,128)(2,1)S(1)}, bf16[512,128]{1,0:T(8,128)(2,1)S(1)}, u32[]{:S(2)}, u32[]{:S(2)}) collective-permute-start(bf16[512,128]{1,0:T(8,128)(2,1)S(1)} %constant_dynamic-slice_fusion), channel_id=1, source_target_pairs={{0,1},{1,0},{2,3},{3,2},{4,5},{5,4},{6,7},{7,6},{8,9},{9,8},{10,11... | collective-permute-start | bytes 393224 | tf_op jit(solution)/shard_map/ppermute | solution.py:24
  25.3 13.9 %collective-permute-start.5 = (bf16[256,1024]{1,0:T(8,128)(2,1)S(1)}, bf16[256,1024]{1,0:T(8,128)(2,1)S(1)}, u32[]{:S(2)}, u32[]{:S(2)}) collective-permute-start(bf16[256,1024]{1,0:T(8,128)(2,1)S(1)} %copy-done.7), channel_id=1, source_target_pairs={{0,256},{256,0},{1,257},{257,1},{2,258},{258,2},{3,259},{259,3},{4... | collective-permute-start | bytes 1572872 | tf_op jit(solution)/shard_map/ppermute | solution.py:24
  28.4 17.1 %collective-permute-start.3 = (bf16[512,256]{1,0:T(8,128)(2,1)S(1)}, bf16[512,256]{1,0:T(8,128)(2,1)S(1)}, u32[]{:S(2)}, u32[]{:S(2)}) collective-permute-start(bf16[512,256]{1,0:T(8,128)(2,1)S(1)} %pad_maximum_fusion.2), channel_id=1, source_target_pairs={{6,0},{0,2},{2,4},{4,6},{7,1},{1,3},{3,5},{5,7},{14,8},{8,10},{10,... | collective-permute-start | bytes 786440 | tf_op jit(solution)/shard_map/ppermute | solution.py:29
  31.6 13.9 %collective-permute-start.2 = (bf16[512,256]{1,0:T(8,128)(2,1)S(1)}, bf16[512,256]{1,0:T(8,128)(2,1)S(1)}, u32[]{:S(2)}, u32[]{:S(2)}) collective-permute-start(bf16[512,256]{1,0:T(8,128)(2,1)S(1)} %pad_maximum_fusion.2), channel_id=1, source_target_pairs={{4,0},{6,2},{0,4},{2,6},{5,1},{7,3},{1,5},{3,7},{12,8},{14,10},{8,... | collective-permute-start | bytes 786440 | tf_op jit(solution)/shard_map/ppermute | solution.py:29
  36.1 10.2 %collective-permute-start.1 = (bf16[512,256]{1,0:T(8,128)(2,1)S(1)}, bf16[512,256]{1,0:T(8,128)(2,1)S(1)}, u32[]{:S(2)}, u32[]{:S(2)}) collective-permute-start(bf16[512,256]{1,0:T(8,128)(2,1)S(1)} %pad_maximum_fusion.2), channel_id=1, source_target_pairs={{2,0},{4,2},{6,4},{0,6},{3,1},{5,3},{7,5},{1,7},{10,8},{12,10},{14... | collective-permute-start | bytes 786440 | tf_op jit(solution)/shard_map/ppermute | solution.py:29
  39.1 7.3 %copy-start.8 = (bf16[256,1024]{1,0:T(8,128)(2,1)}, bf16[256,1024]{1,0:T(8,128)(2,1)S(1)}, u32[]{:S(2)}) copy-start(bf16[256,1024]{1,0:T(8,128)(2,1)S(1)} %collective-permute-done.5) | copy-start | bytes 1572868
  40.3 11.6 %collective-permute-start.6 = (bf16[512,1024]{1,0:T(8,128)(2,1)}, bf16[512,1024]{1,0:T(8,128)(2,1)}, u32[]{:S(2)}, u32[]{:S(2)}) collective-permute-start(bf16[512,1024]{1,0:T(8,128)(2,1)} %pad_maximum_fusion.1), channel_id=1, source_target_pairs={{0,8},{8,0},{1,9},{9,1},{2,10},{10,2},{3,11},{11,3},{4,12},{12,4},... | collective-permute-start | bytes 3145736 | tf_op jit(solution)/shard_map/ppermute | solution.py:24
  46.5 6.8 %copy-start.1 = (bf16[4,512,256]{2,1,0:T(8,128)(2,1)}, bf16[4,512,256]{2,1,0:T(8,128)(2,1)S(1)}, u32[]{:S(2)}) copy-start(bf16[4,512,256]{2,1,0:T(8,128)(2,1)S(1)} %pad_maximum_fusion.near_ref) | copy-start | bytes 3145732
  46.5 6.8 %collective-permute-start.4 = (bf16[4,512,256]{2,1,0:T(8,128)(2,1)S(1)}, bf16[4,512,256]{2,1,0:T(8,128)(2,1)}, u32[]{:S(2)}, u32[]{:S(2)}) collective-permute-start(bf16[4,512,256]{2,1,0:T(8,128)(2,1)S(1)} %pad_maximum_fusion.near_ref), channel_id=1, source_target_pairs={{0,8},{8,0},{1,9},{9,1},{2,10},{10,2},{3,11},{11,3},{4,12},{12,4},... | collective-permute-start | bytes 3145736 | tf_op jit(solution)/shard_map/ppermute | solution.py:24
  57.6 1.4 copy-start.2
  58.9 1.3 copy-start.4
  62.8 3.2 %copy-start.5 = (bf16[1024,1024]{1,0:T(8,128)(2,1)S(1)}, bf16[1024,1024]{1,0:T(8,128)(2,1)}, u32[]{:S(2)}) copy-start(bf16[1024,1024]{1,0:T(8,128)(2,1)} %copy-done.4) | copy-start | bytes 6291460
  67.4 42.2 %copy-start.10 = (s32[256]{0:T(256)S(1)}, s32[256]{0:T(256)}, u32[]{:S(2)}) copy-start(s32[256]{0:T(256)} %param.7) | copy-start | bytes 3076
  109.6 3.6 %copy-start.6 = (bf16[1024,1024]{1,0:T(8,128)(2,1)S(1)}, bf16[1024,1024]{1,0:T(8,128)(2,1)}, u32[]{:S(2)}) copy-start(bf16[1024,1024]{1,0:T(8,128)(2,1)} %copy-done.4) | copy-start | bytes 6291460
  113.2 1.6 copy-start.3
  119.7 6.1 %collective-permute-start.7 = (f32[512,1024]{1,0:T(8,128)S(1)}, f32[512,1024]{1,0:T(8,128)S(1)}, u32[]{:S(2)}, u32[]{:S(2)}) collective-permute-start(f32[512,1024]{1,0:T(8,128)S(1)} %add_add_fusion), channel_id=1, source_target_pairs={{0,8},{8,0},{1,9},{9,1},{2,10},{10,2},{3,11},{11,3},{4,12},{12,4},... | collective-permute-start | bytes 6291464 | tf_op jit(solution)/shard_map/ppermute | solution.py:24

commit v6 on v5

--- a/solution.py
+++ b/solution.py
@@ -64,7 +64,7 @@
     rows, depth = x.shape
     width = near.shape[0] * near.shape[2]
     at = jnp.stack([lax.axis_index("y"), lax.axis_index("core")]).astype(jnp.int32)
-    block = 256
+    block = 512
     return pl.pallas_call(
         project_kernel,
         grid=(rows // block,),
@@ -81,7 +81,7 @@
             bytes_accessed=2 * (rows * depth + depth * width + rows * width),
             transcendentals=0,
         ),
-        compiler_params=pltpu.CompilerParams(vmem_limit_bytes=8 * 2**20),
+        compiler_params=pltpu.CompilerParams(vmem_limit_bytes=14 * 2**20),
     )(at, x, near, far)
 
 

time: 193 us -> 192 us (level)
  no operation moved by 1% of the time
where the time goes in v6:
time: 192 us
  blocking collectives  104 us (54%)
  starting transfers between devices  45.8 us (24%)
  matrix products  14.9 us (8%)
  local copies, waits for them, and re-layouts  9.09 us (5%)
  waiting for transfers between devices  7.4 us (4%)
  Pallas kernels  6.9 us (4%)
  other arithmetic  2.71 us (1%)
    all_to_all x6, blocking collectives, exchange(): return lax.all_to_all(x, axes, split_axis=0, concat_axis=0, tiled=True)  104 us
    ppermute x5, starting transfers between devices, from_twin(): return lax.ppermute(x, axis, [(0, 1), (1, 0)])  19.4 us
    all_to_all x1, starting transfers between devices, exchange(): return lax.all_to_all(x, axes, split_axis=0, concat_axis=0, tiled=True)  15.7 us
    ppermute x3, starting transfers between devices, from_ahead(): lax.ppermute(x, axis, [((i + by) % devices, i) for i in range(devices)])  10.7 us
    dot_general x8, matrix products, dot_first(): lax.dot_general(a, b, (((0,), (0,)), ((), ())), preferred_element_type=jn...  7.34 us
    pallas_call x2, Pallas kernels, project(): pl.pallas_call(project_kernel, grid=(rows // block,), out_shape=jax.Shape...  6.9 us
    unnamed x27, local copies, waits for them, and re-layouts  6.2 us
    dot_general x2, matrix products, score(): lax.dot_general(refusal_emb, prompt_emb, (((1,), (1,)), ((), ())), prefer...  4.99 us
  transfers between devices with their start and end apart: 9, of which 4 were waited for; matrix products, arithmetic and copies ran while one was open for 3% of the time, Pallas kernels for 2%

profile of v6, /device:TPU:1, one launch (start us, length us, event | category | flops | bytes accessed | tf_op | source)
XLA Modules:
  0.0 191.6 jit_solution(1988286429203953850)
XLA Ops:
  0.0 1.0 copy-done
  1.1 1.1 broadcast_in_dim.15
  2.2 15.7 %all-to-all-start = ((bf16[16,32,1024]{2,1,0:T(8,128)(2,1)}), bf16[16,32,1024]{2,1,0:T(8,128)(2,1)S(1)}, u32[]{:S(2)}, u32[]{:S(2)}) async-start(bf16[16,32,1024]{2,1,0:T(8,128)(2,1)} %broadcast_in_dim.15), calls=%async_computation | async-start | bytes 2097152 | tf_op jit(solution)/shard_map/all_to_all | solution.py:16
  17.9 4.7 %collective-permute-start = (bf16[512,128]{1,0:T(8,128)(2,1)S(1)}, bf16[512,128]{1,0:T(8,128)(2,1)S(1)}, u32[]{:S(2)}, u32[]{:S(2)}) collective-permute-start(bf16[512,128]{1,0:T(8,128)(2,1)S(1)} %constant_dynamic-slice_fusion), channel_id=1, source_target_pairs={{0,1},{1,0},{2,3},{3,2},{4,5},{5,4},{6,7},{7,6},{8,9},{9,8},{10,11... | collective-permute-start | bytes 393224 | tf_op jit(solution)/shard_map/ppermute | solution.py:24
  22.6 2.6 %collective-permute-done = bf16[512,128]{1,0:T(8,128)(2,1)S(1)} collective-permute-done((bf16[512,128]{1,0:T(8,128)(2,1)S(1)}, bf16[512,128]{1,0:T(8,128)(2,1)S(1)}, u32[]{:S(2)}, u32[]{:S(2)}) %collective-permute-start) | collective-permute-done | bytes 131104 | tf_op jit(solution)/shard_map/ppermute | solution.py:24
  25.3 3.1 %collective-permute-start.5 = (bf16[256,1024]{1,0:T(8,128)(2,1)S(1)}, bf16[256,1024]{1,0:T(8,128)(2,1)S(1)}, u32[]{:S(2)}, u32[]{:S(2)}) collective-permute-start(bf16[256,1024]{1,0:T(8,128)(2,1)S(1)} %copy-done.7), channel_id=1, source_target_pairs={{0,256},{256,0},{1,257},{257,1},{2,258},{258,2},{3,259},{259,3},{4... | collective-permute-start | bytes 1572872 | tf_op jit(solution)/shard_map/ppermute | solution.py:24
  28.4 3.2 %collective-permute-start.3 = (bf16[512,256]{1,0:T(8,128)(2,1)S(1)}, bf16[512,256]{1,0:T(8,128)(2,1)S(1)}, u32[]{:S(2)}, u32[]{:S(2)}) collective-permute-start(bf16[512,256]{1,0:T(8,128)(2,1)S(1)} %pad_maximum_fusion.2), channel_id=1, source_target_pairs={{6,0},{0,2},{2,4},{4,6},{7,1},{1,3},{3,5},{5,7},{14,8},{8,10},{10,... | collective-permute-start | bytes 786440 | tf_op jit(solution)/shard_map/ppermute | solution.py:29
  31.6 4.5 %collective-permute-start.2 = (bf16[512,256]{1,0:T(8,128)(2,1)S(1)}, bf16[512,256]{1,0:T(8,128)(2,1)S(1)}, u32[]{:S(2)}, u32[]{:S(2)}) collective-permute-start(bf16[512,256]{1,0:T(8,128)(2,1)S(1)} %pad_maximum_fusion.2), channel_id=1, source_target_pairs={{4,0},{6,2},{0,4},{2,6},{5,1},{7,3},{1,5},{3,7},{12,8},{14,10},{8,... | collective-permute-start | bytes 786440 | tf_op jit(solution)/shard_map/ppermute | solution.py:29
  36.1 3.0 %collective-permute-start.1 = (bf16[512,256]{1,0:T(8,128)(2,1)S(1)}, bf16[512,256]{1,0:T(8,128)(2,1)S(1)}, u32[]{:S(2)}, u32[]{:S(2)}) collective-permute-start(bf16[512,256]{1,0:T(8,128)(2,1)S(1)} %pad_maximum_fusion.2), channel_id=1, source_target_pairs={{2,0},{4,2},{6,4},{0,6},{3,1},{5,3},{7,5},{1,7},{10,8},{12,10},{14... | collective-permute-start | bytes 786440 | tf_op jit(solution)/shard_map/ppermute | solution.py:29
  39.2 1.2 pad_maximum_fusion.1
  40.3 5.1 %collective-permute-start.6 = (bf16[512,1024]{1,0:T(8,128)(2,1)}, bf16[512,1024]{1,0:T(8,128)(2,1)}, u32[]{:S(2)}, u32[]{:S(2)}) collective-permute-start(bf16[512,1024]{1,0:T(8,128)(2,1)} %pad_maximum_fusion.1), channel_id=1, source_target_pairs={{0,8},{8,0},{1,9},{9,1},{2,10},{10,2},{3,11},{11,3},{4,12},{12,4},... | collective-permute-start | bytes 3145736 | tf_op jit(solution)/shard_map/ppermute | solution.py:24
  46.5 4.2 %collective-permute-start.4 = (bf16[4,512,256]{2,1,0:T(8,128)(2,1)S(1)}, bf16[4,512,256]{2,1,0:T(8,128)(2,1)}, u32[]{:S(2)}, u32[]{:S(2)}) collective-permute-start(bf16[4,512,256]{2,1,0:T(8,128)(2,1)S(1)} %pad_maximum_fusion.near_ref), channel_id=1, source_target_pairs={{0,8},{8,0},{1,9},{9,1},{2,10},{10,2},{3,11},{11,3},{4,12},{12,4},... | collective-permute-start | bytes 3145736 | tf_op jit(solution)/shard_map/ppermute | solution.py:24
  50.9 1.1 constant_dynamic-update-slice_fusion.1
  52.0 1.3 constant_dynamic-update-slice_fusion.x_ref
  53.3 4.0 %shard_map.47 = bf16[1024,1024]{1,0:T(8,128)(2,1)S(1)} custom-call(s32[2]{0:T(128)S(1)} %pad_add_fusion.at_ref, bf16[1024,1024]{1,0:T(8,128)(2,1)S(1)} %constant_dynamic-update-slice_fusion.x_ref, bf16[4,512,256]{2,1,0:T(8,128)(2,1)S(1)} %pad_maximum_fusion.near_ref, bf16[4,512,256]{2,1,0:T(8,128)(2,1)} %collective-permute-done.4.far_ref), custom_call_target="tpu_custom_call" | custom-call | flops 2147483648 | bytes 6291456 | tf_op jit(solution)/shard_map/pallas_call | solution.py:68
  57.3 1.3 copy-done.2
  58.6 1.3 copy-done.4
  59.9 2.9 %all-to-all-done = bf16[16,32,1024]{2,1,0:T(8,128)(2,1)S(1)} async-done(((bf16[16,32,1024]{2,1,0:T(8,128)(2,1)}), bf16[16,32,1024]{2,1,0:T(8,128)(2,1)S(1)}, u32[]{:S(2)}, u32[]{:S(2)}) %all-to-all-start) | async-done | bytes 1048608 | tf_op jit(solution)/shard_map/all_to_all | solution.py:16
  62.8 2.9 %shard_map.46 = bf16[512,1024]{1,0:T(8,128)(2,1)S(1)} custom-call(s32[2]{0:T(128)S(1)} %pad_add_fusion.at_ref, bf16[512,1024]{1,0:T(8,128)(2,1)S(1)} %bitcast.37, bf16[4,512,256]{2,1,0:T(8,128)(2,1)} %copy-done.1, bf16[4,512,256]{2,1,0:T(8,128)(2,1)} %collective-permute-done.4.far_ref), custom_call_target="tpu_custom_call" | custom-call | flops 1073741824 | bytes 4194304 | tf_op jit(solution)/shard_map/pallas_call | solution.py:68
  65.7 1.4 multiply_reduce_fusion
  68.2 24.5 %all_to_all.35 = f32[16,4,128]{2,1,0:T(4,128)S(1)} all-to-all(f32[16,4,128]{2,1,0:T(4,128)S(1)} %broadcast_in_dim.16), channel_id=1, replica_groups=mesh['x_lo'=2,'z_hi'=4,'z_lo'=4,'core'=2,'y'=4,'x_hi'=2] {'z_hi','z_lo'}, dimensions={0} | all-to-all | bytes 65536 | tf_op jit(solution)/shard_map/all_to_all | solution.py:16
  92.6 16.3 %all_to_all.36 = f32[32,8,128]{2,1,0:T(8,128)S(1)} all-to-all(f32[32,8,128]{2,1,0:T(8,128)S(1)} %broadcast_in_dim.17), channel_id=1, replica_groups=mesh['x_lo'=2,'z_hi'=4,'z_lo'=4,'core'=2,'y'=4,'x_hi'=2] {'core','x_lo',..., dimensions={0} | all-to-all | bytes 262144 | tf_op jit(solution)/shard_map/all_to_all | solution.py:16
  109.4 3.6 %multiply_convert_fusion = bf16[512,1024]{1,0:T(8,128)(2,1)S(1)} fusion(bf16[512,1024]{1,0:T(8,128)(2,1)S(1)} %shard_map.46, bf16[1024,1024]{1,0:T(8,128)(2,1)} %copy-done.4, s32[1024]{0:T(1024)S(1)} %concatenate.16, f32[512]{0:T(512)S(1)} %get-tuple-element.26, f32[1024]{0:T(1024)S(1)} %bitcast.51, s32[512]{0:T(512)S(1)} %get-tuple-element.25), kind=kOutput, calls=%fused_computation.9 | convolution fusion | flops 1078460416 | bytes 4206592 | tf_op jit(solution)/shard_map/dot_general | solution.py:109
  113.0 1.3 fusion.36
  114.6 1.3 fusion
  119.5 2.3 %collective-permute-start.7 = (f32[512,1024]{1,0:T(8,128)S(1)}, f32[512,1024]{1,0:T(8,128)S(1)}, u32[]{:S(2)}, u32[]{:S(2)}) collective-permute-start(f32[512,1024]{1,0:T(8,128)S(1)} %add_add_fusion), channel_id=1, source_target_pairs={{0,8},{8,0},{1,9},{9,1},{2,10},{10,2},{3,11},{11,3},{4,12},{12,4},... | collective-permute-start | bytes 6291464 | tf_op jit(solution)/shard_map/ppermute | solution.py:24
  124.4 1.1 collective-permute-done.7
  125.5 1.1 fusion.2
  127.1 18.2 %all_to_all.37 = bf16[16,256,128]{2,1,0:T(8,128)(2,1)S(1)} all-to-all(bf16[16,256,128]{2,1,0:T(8,128)(2,1)S(1)} %bitcast.43), channel_id=1, replica_groups=mesh['x_lo'=2,'z_hi'=4,'z_lo'=4,'core'=2,'y'=4,'x_hi'=2] {'x_lo','y','x_..., dimensions={0} | all-to-all | bytes 2097152 | tf_op jit(solution)/shard_map/all_to_all | solution.py:16
  145.4 14.6 %all_to_all.38 = f32[16,16,128]{2,1,0:T(8,128)S(1)} all-to-all(f32[16,16,128]{2,1,0:T(8,128)S(1)} %bitcast.46), channel_id=1, replica_groups=mesh['x_lo'=2,'z_hi'=4,'z_lo'=4,'core'=2,'y'=4,'x_hi'=2] {'z_hi','z_lo'}, dimensions={0} | all-to-all | bytes 262144 | tf_op jit(solution)/shard_map/all_to_all | solution.py:16
  160.0 15.7 %all_to_all.39 = f32[16,16,128]{2,1,0:T(8,128)S(1)} all-to-all(f32[16,16,128]{2,1,0:T(8,128)S(1)} %broadcast_in_dim.20), channel_id=1, replica_groups=mesh['x_lo'=2,'z_hi'=4,'z_lo'=4,'core'=2,'y'=4,'x_hi'=2] {'z_hi','z_lo'}, dimensions={0} | all-to-all | bytes 262144 | tf_op jit(solution)/shard_map/all_to_all | solution.py:16
  175.8 15.0 %all_to_all.40 = f32[4,256,128]{2,1,0:T(8,128)S(1)} all-to-all(f32[4,256,128]{2,1,0:T(8,128)S(1)} %broadcast_in_dim.22), channel_id=1, replica_groups=mesh['x_lo'=2,'z_hi'=4,'z_lo'=4,'core'=2,'y'=4,'x_hi'=2] {'core','x_lo'}, dimensions={0} | all-to-all | bytes 1048576 | tf_op jit(solution)/shard_map/all_to_all | solution.py:16
  (69 shorter events, 10.6 us)
Async XLA Ops:
  0.0 1.0 copy-start
  0.0 17.9 %copy-start.9 = (bf16[1024,128]{1,0:T(8,128)(2,1)S(1)}, bf16[1024,128]{1,0:T(8,128)(2,1)}, u32[]{:S(2)}) copy-start(bf16[1024,128]{1,0:T(8,128)(2,1)} %param.6) | copy-start | bytes 786436
  1.0 24.2 %copy-start.7 = (bf16[256,1024]{1,0:T(8,128)(2,1)S(1)}, bf16[256,1024]{1,0:T(8,128)(2,1)}, u32[]{:S(2)}) copy-start(bf16[256,1024]{1,0:T(8,128)(2,1)} %param.4) | copy-start | bytes 1572868
  2.2 60.6 %all-to-all-start = ((bf16[16,32,1024]{2,1,0:T(8,128)(2,1)}), bf16[16,32,1024]{2,1,0:T(8,128)(2,1)S(1)}, u32[]{:S(2)}, u32[]{:S(2)}) async-start(bf16[16,32,1024]{2,1,0:T(8,128)(2,1)} %broadcast_in_dim.15), calls=%async_computation | async-start | bytes 2097152 | tf_op jit(solution)/shard_map/all_to_all | solution.py:16
  17.9 7.2 %collective-permute-start = (bf16[512,128]{1,0:T(8,128)(2,1)S(1)}, bf16[512,128]{1,0:T(8,128)(2,1)S(1)}, u32[]{:S(2)}, u32[]{:S(2)}) collective-permute-start(bf16[512,128]{1,0:T(8,128)(2,1)S(1)} %constant_dynamic-slice_fusion), channel_id=1, source_target_pairs={{0,1},{1,0},{2,3},{3,2},{4,5},{5,4},{6,7},{7,6},{8,9},{9,8},{10,11... | collective-permute-start | bytes 393224 | tf_op jit(solution)/shard_map/ppermute | solution.py:24
  25.3 13.9 %collective-permute-start.5 = (bf16[256,1024]{1,0:T(8,128)(2,1)S(1)}, bf16[256,1024]{1,0:T(8,128)(2,1)S(1)}, u32[]{:S(2)}, u32[]{:S(2)}) collective-permute-start(bf16[256,1024]{1,0:T(8,128)(2,1)S(1)} %copy-done.7), channel_id=1, source_target_pairs={{0,256},{256,0},{1,257},{257,1},{2,258},{258,2},{3,259},{259,3},{4... | collective-permute-start | bytes 1572872 | tf_op jit(solution)/shard_map/ppermute | solution.py:24
  28.4 17.1 %collective-permute-start.3 = (bf16[512,256]{1,0:T(8,128)(2,1)S(1)}, bf16[512,256]{1,0:T(8,128)(2,1)S(1)}, u32[]{:S(2)}, u32[]{:S(2)}) collective-permute-start(bf16[512,256]{1,0:T(8,128)(2,1)S(1)} %pad_maximum_fusion.2), channel_id=1, source_target_pairs={{6,0},{0,2},{2,4},{4,6},{7,1},{1,3},{3,5},{5,7},{14,8},{8,10},{10,... | collective-permute-start | bytes 786440 | tf_op jit(solution)/shard_map/ppermute | solution.py:29
  31.6 13.9 %collective-permute-start.2 = (bf16[512,256]{1,0:T(8,128)(2,1)S(1)}, bf16[512,256]{1,0:T(8,128)(2,1)S(1)}, u32[]{:S(2)}, u32[]{:S(2)}) collective-permute-start(bf16[512,256]{1,0:T(8,128)(2,1)S(1)} %pad_maximum_fusion.2), channel_id=1, source_target_pairs={{4,0},{6,2},{0,4},{2,6},{5,1},{7,3},{1,5},{3,7},{12,8},{14,10},{8,... | collective-permute-start | bytes 786440 | tf_op jit(solution)/shard_map/ppermute | solution.py:29
  36.1 10.2 %collective-permute-start.1 = (bf16[512,256]{1,0:T(8,128)(2,1)S(1)}, bf16[512,256]{1,0:T(8,128)(2,1)S(1)}, u32[]{:S(2)}, u32[]{:S(2)}) collective-permute-start(bf16[512,256]{1,0:T(8,128)(2,1)S(1)} %pad_maximum_fusion.2), channel_id=1, source_target_pairs={{2,0},{4,2},{6,4},{0,6},{3,1},{5,3},{7,5},{1,7},{10,8},{12,10},{14... | collective-permute-start | bytes 786440 | tf_op jit(solution)/shard_map/ppermute | solution.py:29
  39.1 7.3 %copy-start.8 = (bf16[256,1024]{1,0:T(8,128)(2,1)}, bf16[256,1024]{1,0:T(8,128)(2,1)S(1)}, u32[]{:S(2)}) copy-start(bf16[256,1024]{1,0:T(8,128)(2,1)S(1)} %collective-permute-done.5) | copy-start | bytes 1572868
  40.3 11.6 %collective-permute-start.6 = (bf16[512,1024]{1,0:T(8,128)(2,1)}, bf16[512,1024]{1,0:T(8,128)(2,1)}, u32[]{:S(2)}, u32[]{:S(2)}) collective-permute-start(bf16[512,1024]{1,0:T(8,128)(2,1)} %pad_maximum_fusion.1), channel_id=1, source_target_pairs={{0,8},{8,0},{1,9},{9,1},{2,10},{10,2},{3,11},{11,3},{4,12},{12,4},... | collective-permute-start | bytes 3145736 | tf_op jit(solution)/shard_map/ppermute | solution.py:24
  46.5 6.8 %copy-start.1 = (bf16[4,512,256]{2,1,0:T(8,128)(2,1)}, bf16[4,512,256]{2,1,0:T(8,128)(2,1)S(1)}, u32[]{:S(2)}) copy-start(bf16[4,512,256]{2,1,0:T(8,128)(2,1)S(1)} %pad_maximum_fusion.near_ref) | copy-start | bytes 3145732
  46.5 6.8 %collective-permute-start.4 = (bf16[4,512,256]{2,1,0:T(8,128)(2,1)S(1)}, bf16[4,512,256]{2,1,0:T(8,128)(2,1)}, u32[]{:S(2)}, u32[]{:S(2)}) collective-permute-start(bf16[4,512,256]{2,1,0:T(8,128)(2,1)S(1)} %pad_maximum_fusion.near_ref), channel_id=1, source_target_pairs={{0,8},{8,0},{1,9},{9,1},{2,10},{10,2},{3,11},{11,3},{4,12},{12,4},... | collective-permute-start | bytes 3145736 | tf_op jit(solution)/shard_map/ppermute | solution.py:24
  57.2 1.4 copy-start.2
  58.6 1.3 copy-start.4
  62.8 3.0 %copy-start.5 = (bf16[1024,1024]{1,0:T(8,128)(2,1)S(1)}, bf16[1024,1024]{1,0:T(8,128)(2,1)}, u32[]{:S(2)}) copy-start(bf16[1024,1024]{1,0:T(8,128)(2,1)} %copy-done.4) | copy-start | bytes 6291460
  67.1 42.2 %copy-start.10 = (s32[256]{0:T(256)S(1)}, s32[256]{0:T(256)}, u32[]{:S(2)}) copy-start(s32[256]{0:T(256)} %param.7) | copy-start | bytes 3076
  109.3 3.6 %copy-start.6 = (bf16[1024,1024]{1,0:T(8,128)(2,1)S(1)}, bf16[1024,1024]{1,0:T(8,128)(2,1)}, u32[]{:S(2)}) copy-start(bf16[1024,1024]{1,0:T(8,128)(2,1)} %copy-done.4) | copy-start | bytes 6291460
  113.0 1.6 copy-start.3
  119.5 6.1 %collective-permute-start.7 = (f32[512,1024]{1,0:T(8,128)S(1)}, f32[512,1024]{1,0:T(8,128)S(1)}, u32[]{:S(2)}, u32[]{:S(2)}) collective-permute-start(f32[512,1024]{1,0:T(8,128)S(1)} %add_add_fusion), channel_id=1, source_target_pairs={{0,8},{8,0},{1,9},{9,1},{2,10},{10,2},{3,11},{11,3},{4,12},{12,4},... | collective-permute-start | bytes 6291464 | tf_op jit(solution)/shard_map/ppermute | solution.py:24
